TPU v7x, 32 devices: a whole 2x2x4 slice. The times are simulated.
32 devices in a mesh: seq: 8 (over y, x, core), vocab: 4 (over z).
Axes of the slice: x: 2, y: 2, z: 4, core: 2. Of those that a mesh axis runs over, the one named last changes fastest.
Arguments:
- policy_hidden: bfloat16 [2048, 2560], P('seq'), may hold values from -45 to 45
- reference_hidden: bfloat16 [2048, 2560], P('seq'), may hold values from -45 to 45
- targets: int32 [2048], P('seq'), may hold values from 0 to 2559
- lengths: int32 [4], replicated, may hold values from 1 to 1024, 2048 in all
- block_source: int32 [16], P('seq'), may hold values from 0 to 15, each once
- rollout_prompt: int32 [4], replicated, may hold values from 0 to 3, each once
- rollout_slot: int32 [4], replicated, may hold values from 0 to 3, each once
- policy_input_gain: float32 [2560], replicated, may hold values from 0.3 to 3
- policy_query_weight: bfloat16 [2560, 2048], P(None, 'vocab'), may hold values from -0.125 to 0.125
- policy_key_weight: bfloat16 [2560, 512], P(None, 'vocab'), may hold values from -0.125 to 0.125
- policy_value_weight: bfloat16 [2560, 512], P(None, 'vocab'), may hold values from -0.125 to 0.125
- policy_query_gain: float32 [128], replicated, may hold values from 0.5 to 9, as said below
- policy_key_gain: float32 [128], replicated, may hold values from 0.5 to 9, as said below
- policy_out_weight: bfloat16 [2048, 2560], P('vocab'), may hold values from -0.5 to 0.5
- policy_final_gain: float32 [2560], replicated, may hold values from 1.5 to 60, as said below
- policy_head: bfloat16 [2560, 2560], P(None, 'vocab'), may hold values from -0.125 to 0.125
- policy_prompt_keys: bfloat16 [4, 64, 512], P(None, 'seq', 'vocab'), may hold values from -6 to 6
- policy_prompt_values: bfloat16 [4, 64, 512], P(None, 'seq', 'vocab'), may hold values from -6 to 6
- reference_input_gain: float32 [2560], replicated, may hold values from 0.3 to 3
- reference_query_weight: bfloat16 [2560, 2048], P(None, 'vocab'), may hold values from -0.125 to 0.125
- reference_key_weight: bfloat16 [2560, 512], P(None, 'vocab'), may hold values from -0.125 to 0.125
- reference_value_weight: bfloat16 [2560, 512], P(None, 'vocab'), may hold values from -0.125 to 0.125
- reference_query_gain: float32 [128], replicated, may hold values from 0.5 to 9, as said below
- reference_key_gain: float32 [128], replicated, may hold values from 0.5 to 9, as said below
- reference_out_weight: bfloat16 [2048, 2560], P('vocab'), may hold values from -0.5 to 0.5
- reference_final_gain: float32 [2560], replicated, may hold values from 1.5 to 60, as said below
- reference_head: bfloat16 [2560, 2560], P(None, 'vocab'), may hold values from -0.125 to 0.125
- reference_prompt_keys: bfloat16 [4, 64, 512], P(None, 'seq', 'vocab'), may hold values from -6 to 6
- reference_prompt_values: bfloat16 [4, 64, 512], P(None, 'seq', 'vocab'), may hold values from -6 to 6
Outputs:
- token_diff: float32 [2048], P('seq')
- rollout_mean: float32 [4], replicated
Inputs may be any that keep to these rules, and one draw needn't show every extreme that they name: `policy_query_gain`: positive. `policy_key_gain`: positive. `reference_query_gain`: positive. `reference_key_gain`: positive. `policy_final_gain`: positive. `reference_final_gain`: positive.
All inputs are finite; a program needn't handle non-finite values.
Results may differ from a plain program's by a relative error of at most 0.04.
The roundings to bfloat16 on the way count: a program that leaves them out, or rounds other values in their place, can miss the bound.
Values may be sent and summed in bfloat16 or wider, within the bound.
A program may use at most 128 MiB of HBM per device.

v0:
```python
import jax
import jax.numpy as jnp
from jax import lax
from jax.sharding import PartitionSpec as P

HD = 128
BLOCK = 128


EPSILON = 1e-06
ROPE_BASE = 1000000.0
NEGATIVE_FILL = -1e30


def rms_scale(values, gain_row):
    values = values.astype(jnp.float32)
    return (
        values * lax.rsqrt(jnp.mean(values * values, axis=-1, keepdims=True) + EPSILON) * gain_row
    )


def rotate(values, positions):
    half_width = values.shape[-1] // 2
    frequency = ROPE_BASE ** (-2.0 * jnp.arange(half_width, dtype=jnp.float32) / values.shape[-1])
    angles = positions.astype(jnp.float32)[:, None] * frequency[None, :]
    cosine = jnp.cos(angles)
    sine_part = jnp.sin(angles)
    cosine = jnp.concatenate([cosine, cosine], axis=-1)[:, None, :]
    sine_part = jnp.concatenate([sine_part, sine_part], axis=-1)[:, None, :]
    turned = jnp.concatenate([-values[..., half_width:], values[..., :half_width]], axis=-1)
    return values * cosine + turned * sine_part


def lookup(member, lookup_table):
    return jnp.sum(jnp.where(member, lookup_table[None, :], 0), axis=1)


def project(
    hidden,
    input_gain,
    query_weight,
    key_weight,
    value_weight,
    query_gain,
    key_gain,
    prompt_keys,
    prompt_values,
    positions,
    rope_offset,
):
    tok_rows = hidden.shape[0]
    kv_local = key_weight.shape[1] // HD
    normed = rms_scale(hidden, input_gain).astype(jnp.bfloat16)
    query_rows = jnp.dot(normed, query_weight, preferred_element_type=jnp.float32).reshape(
        tok_rows, -1, HD
    )
    query_rows = rotate(rms_scale(query_rows, query_gain), positions + rope_offset).astype(
        jnp.bfloat16
    )
    key_rows = jnp.dot(normed, key_weight, preferred_element_type=jnp.float32).reshape(
        tok_rows, kv_local, HD
    )
    key_rows = (
        rotate(rms_scale(key_rows, key_gain), positions + rope_offset)
        .astype(jnp.bfloat16)
        .reshape(tok_rows, kv_local * HD)
    )
    value_rows = jnp.dot(normed, value_weight, preferred_element_type=jnp.float32).astype(
        jnp.bfloat16
    )
    key_block = jnp.concatenate([key_rows, prompt_keys.reshape(-1, kv_local * HD)], axis=0)
    value_block = jnp.concatenate([value_rows, prompt_values.reshape(-1, kv_local * HD)], axis=0)
    stacked = jnp.concatenate([key_block, value_block], axis=1)
    return (query_rows.reshape(tok_rows, kv_local, -1, HD), stacked)


def empty_state(query_rows):
    tok_rows, kv_local, group_size = (query_rows.shape[0], query_rows.shape[1], query_rows.shape[2])
    running_max = jnp.full((kv_local, group_size, tok_rows), NEGATIVE_FILL, jnp.float32)
    weight_sum = jnp.zeros((kv_local, group_size, tok_rows), jnp.float32)
    accumulated = jnp.zeros((tok_rows, kv_local, group_size, HD), jnp.float32)
    return (running_max, weight_sum, accumulated)


def update_state(model_state, query_rows, stacked, visible):
    running_max, weight_sum, accumulated = model_state
    half_columns = stacked.shape[1] // 2
    kv_local = query_rows.shape[1]
    key_part = stacked[:, :half_columns].reshape(-1, kv_local, HD)
    value_part = stacked[:, half_columns:].reshape(-1, kv_local, HD)
    scores = jnp.einsum(
        "qkgd,skd->kgqs", query_rows, key_part, preferred_element_type=jnp.float32
    ) * HD ** (-0.5)
    masked = jnp.where(visible[None, None], scores, NEGATIVE_FILL)
    new_max = jnp.maximum(running_max, jnp.max(masked, axis=-1))
    weights = jnp.where(visible[None, None], jnp.exp(scores - new_max[..., None]), 0.0)
    factor = jnp.exp(running_max - new_max)
    new_sum = weight_sum * factor + jnp.sum(weights, axis=-1)
    product = jnp.einsum(
        "kgqs,skd->qkgd",
        weights.astype(jnp.bfloat16),
        value_part,
        preferred_element_type=jnp.float32,
    )
    new_accumulated = accumulated * jnp.transpose(factor, (2, 0, 1))[..., None] + product
    return (new_max, new_sum, new_accumulated)


def attend(states, queries, pieces, query_tag, query_position, query_prompt):
    stacked_list = pieces[:-2]
    key_tag = pieces[-2]
    key_position = pieces[-1]
    visible = (key_tag[None, :] == query_tag[:, None]) & (
        key_position[None, :] <= query_position[:, None]
    ) | (key_tag[None, :] == -1 - query_prompt[:, None])

    def compute(current):
        updated = []
        for model_state, query_rows, stacked in zip(current, queries, stacked_list):
            updated.append(update_state(model_state, query_rows, stacked, visible))
        return tuple(updated)

    def unchanged(current):
        return current

    return lax.cond(jnp.any(visible), compute, unchanged, states)


def make_fold(queries, query_tag, query_position, query_prompt, shard_rows):

    def fold_pieces(states, pieces, start_row):
        rows_here = pieces[0].shape[0]
        shard_count = rows_here // shard_rows
        split_pieces = tuple(
            (
                member_piece.reshape((shard_count, shard_rows) + member_piece.shape[1:])
                for member_piece in pieces
            )
        )

        def scan_step(carry_states, piece_item):
            return (
                attend(carry_states, queries, piece_item, query_tag, query_position, query_prompt),
                None,
            )

        return lax.scan(scan_step, states, split_pieces)[0]

    return fold_pieces


def finish(model_state, out_weight):
    running_max, weight_sum, accumulated = model_state
    attended = accumulated / jnp.transpose(weight_sum, (2, 0, 1))[..., None]
    attended = attended.reshape(accumulated.shape[0], -1).astype(jnp.bfloat16)
    return jnp.dot(attended, out_weight, preferred_element_type=jnp.float32)


def head_terms(final_rows, head_weight, targets, vocab_start):
    logits = jnp.dot(final_rows, head_weight, preferred_element_type=jnp.float32)
    local_max = jnp.max(logits, axis=-1)
    word_ids = vocab_start + jnp.arange(logits.shape[1], dtype=jnp.int32)
    target_logit = jnp.sum(jnp.where(word_ids[None, :] == targets[:, None], logits, 0.0), axis=-1)
    return (logits, local_max, target_logit)


def local(
    policy_hidden,
    reference_hidden,
    targets,
    lengths,
    block_source,
    rollout_prompt,
    rollout_slot,
    policy_input_gain,
    policy_query_weight,
    policy_key_weight,
    policy_value_weight,
    policy_query_gain,
    policy_key_gain,
    policy_out_weight,
    policy_final_gain,
    policy_head,
    policy_prompt_keys,
    policy_prompt_values,
    reference_input_gain,
    reference_query_weight,
    reference_key_weight,
    reference_value_weight,
    reference_query_gain,
    reference_key_gain,
    reference_out_weight,
    reference_final_gain,
    reference_head,
    reference_prompt_keys,
    reference_prompt_values,
):
    tok_rows = policy_hidden.shape[0]
    roll_ids = jnp.arange(lengths.shape[0], dtype=jnp.int32)
    slot_ids = jnp.arange(tok_rows, dtype=jnp.int32)
    packed = jnp.repeat(block_source, BLOCK) * BLOCK + slot_ids % BLOCK
    end_points = jnp.cumsum(lengths)
    rollout = jnp.sum((packed[:, None] >= end_points[None, :]).astype(jnp.int32), axis=1)
    member = rollout[:, None] == roll_ids[None, :]
    position = packed - lookup(member, end_points - lengths)
    query_prompt = lookup(member, rollout_prompt)
    slot_of = lookup(member, rollout_slot)
    length_of = lookup(member, lengths)
    prompt_count = policy_prompt_keys.shape[0]
    prefix_local = policy_prompt_keys.shape[1]
    prompt_rows = prompt_count * prefix_local
    rope_offset = prefix_local * lax.axis_size("seq")
    prompt_ids = jnp.arange(prompt_rows, dtype=jnp.int32) // prefix_local
    key_tag = jnp.concatenate([rollout, -1 - prompt_ids])
    key_position = jnp.concatenate([position, jnp.full((prompt_rows,), -1, jnp.int32)])
    shard_rows = tok_rows + prompt_rows
    policy_query, policy_stack = project(
        policy_hidden,
        policy_input_gain,
        policy_query_weight,
        policy_key_weight,
        policy_value_weight,
        policy_query_gain,
        policy_key_gain,
        policy_prompt_keys,
        policy_prompt_values,
        position,
        rope_offset,
    )
    reference_query, reference_stack = project(
        reference_hidden,
        reference_input_gain,
        reference_query_weight,
        reference_key_weight,
        reference_value_weight,
        reference_query_gain,
        reference_key_gain,
        reference_prompt_keys,
        reference_prompt_values,
        position,
        rope_offset,
    )
    fold_policy = make_fold((policy_query,), rollout, position, query_prompt, shard_rows)
    (policy_state,) = fold_policy(
        (empty_state(policy_query),),
        (
            lax.all_gather(policy_stack, "seq", axis=0, tiled=True),
            lax.all_gather(key_tag, "seq", axis=0, tiled=True),
            lax.all_gather(key_position, "seq", axis=0, tiled=True),
        ),
        jnp.int32(0),
    )
    fold_reference = make_fold((reference_query,), rollout, position, query_prompt, shard_rows)
    (reference_state,) = fold_reference(
        (empty_state(reference_query),),
        (
            lax.all_gather(reference_stack, "seq", axis=0, tiled=True),
            lax.all_gather(key_tag, "seq", axis=0, tiled=True),
            lax.all_gather(key_position, "seq", axis=0, tiled=True),
        ),
        jnp.int32(0),
    )
    policy_part = finish(policy_state, policy_out_weight)
    reference_part = finish(reference_state, reference_out_weight)
    policy_mixed, reference_mixed = (
        lax.psum(policy_part.astype(jnp.bfloat16), "vocab").astype(jnp.float32),
        lax.psum(reference_part.astype(jnp.bfloat16), "vocab").astype(jnp.float32),
    )
    policy_final = rms_scale(
        policy_hidden.astype(jnp.float32) + policy_mixed, policy_final_gain
    ).astype(jnp.bfloat16)
    reference_final = rms_scale(
        reference_hidden.astype(jnp.float32) + reference_mixed, reference_final_gain
    ).astype(jnp.bfloat16)
    vocab_start = lax.axis_index("vocab") * policy_head.shape[1]
    policy_logits, policy_max, policy_target = head_terms(
        policy_final, policy_head, targets, vocab_start
    )
    reference_logits, reference_max, reference_target = head_terms(
        reference_final, reference_head, targets, vocab_start
    )
    policy_top, reference_top = lax.pmax((policy_max, reference_max), "vocab")
    policy_local = jnp.sum(jnp.exp(policy_logits - policy_top[:, None]), axis=-1)
    reference_local = jnp.sum(jnp.exp(reference_logits - reference_top[:, None]), axis=-1)
    totals = lax.psum((policy_local, reference_local, policy_target, reference_target), "vocab")
    policy_score = totals[2] - (policy_top + jnp.log(totals[0]))
    reference_score = totals[3] - (reference_top + jnp.log(totals[1]))
    token_diff = policy_score - reference_score
    per_token = token_diff / length_of.astype(jnp.float32)
    partial_sums = jnp.sum(
        jnp.where(slot_of[:, None] == roll_ids[None, :], per_token[:, None], 0.0), axis=0
    )
    rollout_mean = lax.psum(partial_sums, "seq")
    return (token_diff, rollout_mean)


def solution(mesh):
    return jax.shard_map(
        local,
        mesh=mesh,
        in_specs=(
            P("seq", None),
            P("seq", None),
            P("seq"),
            P(),
            P("seq"),
            P(),
            P(),
            P(),
            P(None, "vocab"),
            P(None, "vocab"),
            P(None, "vocab"),
            P(),
            P(),
            P("vocab", None),
            P(),
            P(None, "vocab"),
            P(None, "seq", "vocab"),
            P(None, "seq", "vocab"),
            P(),
            P(None, "vocab"),
            P(None, "vocab"),
            P(None, "vocab"),
            P(),
            P(),
            P("vocab", None),
            P(),
            P(None, "vocab"),
            P(None, "seq", "vocab"),
            P(None, "seq", "vocab"),
        ),
        out_specs=(P("seq"), P()),
        check_vma=False,
    )
```

profile of v0, /device:TPU:0, one launch (start us, length us, event | category | flops | bytes accessed | tf_op | source)
XLA Modules:
  0.0 356.8 jit_solution(11746757903800687421)
XLA Ops:
  32.2 3.9 %fusion.65 = f32[256,512]{1,0:T(8,128)} fusion(bf16[2560,512]{1,0:T(8,128)(2,1)} %param.45, bf16[256,2560]{1,0:T(8,128)(2,1)} %param.37, f32[2560]{0:T(1024)} %param.44, f32[256]{0:T(256)S(1)} %copy-done.32), kind=kOutput, calls=%fused_computation.166 | convolution fusion | flops 673710080 | bytes 4467712 | tf_op jit(solution)/shard_map/dot_general | solution.py:54
  40.1 3.8 %fusion.60 = f32[256,512]{1,0:T(8,128)} fusion(bf16[2560,512]{1,0:T(8,128)(2,1)} %param.56, bf16[256,2560]{1,0:T(8,128)(2,1)} %param.38, f32[2560]{0:T(1024)S(1)} %copy-done.42, f32[256]{0:T(256)S(1)} %copy-done.34), kind=kOutput, calls=%fused_computation.164 | convolution fusion | flops 673710080 | bytes 4467712 | tf_op jit(solution)/shard_map/dot_general | solution.py:54
  43.9 2.0 reshape.431
  49.6 2.1 multiply_reduce_fusion.2
  53.9 2.1 multiply_reduce_fusion.3
  64.8 27.0 %all-reduce.3 = (s32[2304]{0:T(1024)}, s32[2304]{0:T(1024)}) all-reduce(s32[2304]{0:T(1024)} %add_dynamic-update-slice_fusion, s32[2304]{0:T(1024)} %pad_dynamic-update-slice_fusion), channel_id=1, replica_groups=mesh['seq'=8,'vocab'=4] {'seq'}, use_global_device_ids=true, to_apply=%add.1 | all-reduce | flops 4608 | bytes 36864
  100.2 48.5 %while.28 = (s32[]{:T(128)}, f32[1,4,256]{2,1,0:T(4,128)S(1)}, f32[1,4,256]{2,1,0:T(4,128)S(1)}, f32[256,1,4,128]{0,3,2,1:T(8,128)}, s32[8,288]{1,0:T(8,128)}, /...) while((s32[]{:T(128)}, f32[1,4,256]{2,1,0:T(4,128)S(1)}, ...), condition=%wide.region_13.14_spmd, body=%wide.region_7.13_spmd.sunk | while | flops 154356992 | bytes 9859115 | solution.py:147
  102.5 3.7 %conditional.4 = ((f32[1,4,256]{2,1,0:T(4,128)S(1)}, f32[1,4,256]{2,1,0:T(4,128)S(1)}, f32[256,1,4,128]{0,3,2,1:T(8,128)})) conditional(s32[]{:T(128)} %convert_element_type.232, (f32[1,4,256]{2,1,0:T(4,128)S(1)}, f32[1,4,256]{2,1,0:T(4,128)S(1)}, f32[256,1,4,128]{0,3,2,1:T(8,128)}) %tuple.96, (pred[256,288]{0,1:T(8,128)(4,1)S(1)}, ...), branch_computations={%region_9.9_spmd, %region_10.12_spmd} | conditional | flops 153914368 | bytes 9773148 | solution.py:126
  108.6 3.7 %conditional.4 = ((f32[1,4,256]{2,1,0:T(4,128)S(1)}, f32[1,4,256]{2,1,0:T(4,128)S(1)}, f32[256,1,4,128]{0,3,2,1:T(8,128)})) conditional(s32[]{:T(128)} %convert_element_type.232, (f32[1,4,256]{2,1,0:T(4,128)S(1)}, f32[1,4,256]{2,1,0:T(4,128)S(1)}, f32[256,1,4,128]{0,3,2,1:T(8,128)}) %tuple.96, (pred[256,288]{0,1:T(8,128)(4,1)S(1)}, ...), branch_computations={%region_9.9_spmd, %region_10.12_spmd} | conditional | flops 153914368 | bytes 9773148 | solution.py:126
  114.7 3.7 %conditional.4 = ((f32[1,4,256]{2,1,0:T(4,128)S(1)}, f32[1,4,256]{2,1,0:T(4,128)S(1)}, f32[256,1,4,128]{0,3,2,1:T(8,128)})) conditional(s32[]{:T(128)} %convert_element_type.232, (f32[1,4,256]{2,1,0:T(4,128)S(1)}, f32[1,4,256]{2,1,0:T(4,128)S(1)}, f32[256,1,4,128]{0,3,2,1:T(8,128)}) %tuple.96, (pred[256,288]{0,1:T(8,128)(4,1)S(1)}, ...), branch_computations={%region_9.9_spmd, %region_10.12_spmd} | conditional | flops 153914368 | bytes 9773148 | solution.py:126
  120.7 3.7 %conditional.4 = ((f32[1,4,256]{2,1,0:T(4,128)S(1)}, f32[1,4,256]{2,1,0:T(4,128)S(1)}, f32[256,1,4,128]{0,3,2,1:T(8,128)})) conditional(s32[]{:T(128)} %convert_element_type.232, (f32[1,4,256]{2,1,0:T(4,128)S(1)}, f32[1,4,256]{2,1,0:T(4,128)S(1)}, f32[256,1,4,128]{0,3,2,1:T(8,128)}) %tuple.96, (pred[256,288]{0,1:T(8,128)(4,1)S(1)}, ...), branch_computations={%region_9.9_spmd, %region_10.12_spmd} | conditional | flops 153914368 | bytes 9773148 | solution.py:126
  126.8 3.7 %conditional.4 = ((f32[1,4,256]{2,1,0:T(4,128)S(1)}, f32[1,4,256]{2,1,0:T(4,128)S(1)}, f32[256,1,4,128]{0,3,2,1:T(8,128)})) conditional(s32[]{:T(128)} %convert_element_type.232, (f32[1,4,256]{2,1,0:T(4,128)S(1)}, f32[1,4,256]{2,1,0:T(4,128)S(1)}, f32[256,1,4,128]{0,3,2,1:T(8,128)}) %tuple.96, (pred[256,288]{0,1:T(8,128)(4,1)S(1)}, ...), branch_computations={%region_9.9_spmd, %region_10.12_spmd} | conditional | flops 153914368 | bytes 9773148 | solution.py:126
  132.8 3.7 %conditional.4 = ((f32[1,4,256]{2,1,0:T(4,128)S(1)}, f32[1,4,256]{2,1,0:T(4,128)S(1)}, f32[256,1,4,128]{0,3,2,1:T(8,128)})) conditional(s32[]{:T(128)} %convert_element_type.232, (f32[1,4,256]{2,1,0:T(4,128)S(1)}, f32[1,4,256]{2,1,0:T(4,128)S(1)}, f32[256,1,4,128]{0,3,2,1:T(8,128)}) %tuple.96, (pred[256,288]{0,1:T(8,128)(4,1)S(1)}, ...), branch_computations={%region_9.9_spmd, %region_10.12_spmd} | conditional | flops 153914368 | bytes 9773148 | solution.py:126
  138.9 3.7 %conditional.4 = ((f32[1,4,256]{2,1,0:T(4,128)S(1)}, f32[1,4,256]{2,1,0:T(4,128)S(1)}, f32[256,1,4,128]{0,3,2,1:T(8,128)})) conditional(s32[]{:T(128)} %convert_element_type.232, (f32[1,4,256]{2,1,0:T(4,128)S(1)}, f32[1,4,256]{2,1,0:T(4,128)S(1)}, f32[256,1,4,128]{0,3,2,1:T(8,128)}) %tuple.96, (pred[256,288]{0,1:T(8,128)(4,1)S(1)}, ...), branch_computations={%region_9.9_spmd, %region_10.12_spmd} | conditional | flops 153914368 | bytes 9773148 | solution.py:126
  145.0 3.7 %conditional.4 = ((f32[1,4,256]{2,1,0:T(4,128)S(1)}, f32[1,4,256]{2,1,0:T(4,128)S(1)}, f32[256,1,4,128]{0,3,2,1:T(8,128)})) conditional(s32[]{:T(128)} %convert_element_type.232, (f32[1,4,256]{2,1,0:T(4,128)S(1)}, f32[1,4,256]{2,1,0:T(4,128)S(1)}, f32[256,1,4,128]{0,3,2,1:T(8,128)}) %tuple.96, (pred[256,288]{0,1:T(8,128)(4,1)S(1)}, ...), branch_computations={%region_9.9_spmd, %region_10.12_spmd} | conditional | flops 153914368 | bytes 9773148 | solution.py:126
  149.6 47.6 %while.29 = (s32[]{:T(128)}, f32[1,4,256]{2,1,0:T(4,128)S(1)}, f32[1,4,256]{2,1,0:T(4,128)S(1)}, f32[256,1,4,128]{0,3,2,1:T(8,128)}, s32[8,288]{1,0:T(8,128)}, /...) while((s32[]{:T(128)}, f32[1,4,256]{2,1,0:T(4,128)S(1)}, ...), condition=%wide.region_31.32_spmd, body=%wide.region_25.31_spmd.sunk | while | flops 154356992 | bytes 9859115 | solution.py:147
  151.8 3.7 %conditional.5 = ((f32[1,4,256]{2,1,0:T(4,128)S(1)}, f32[1,4,256]{2,1,0:T(4,128)S(1)}, f32[256,1,4,128]{0,3,2,1:T(8,128)})) conditional(s32[]{:T(128)} %convert_element_type.233, (f32[1,4,256]{2,1,0:T(4,128)S(1)}, f32[1,4,256]{2,1,0:T(4,128)S(1)}, f32[256,1,4,128]{0,3,2,1:T(8,128)}) %tuple.101, (pred[256,288]{0,1:T(8,128)(4,1)S(1)}, ...), branch_computations={%region_27.27_spmd, %region_28.30_spmd} | conditional | flops 153914368 | bytes 9773148 | solution.py:126
  157.7 3.7 %conditional.5 = ((f32[1,4,256]{2,1,0:T(4,128)S(1)}, f32[1,4,256]{2,1,0:T(4,128)S(1)}, f32[256,1,4,128]{0,3,2,1:T(8,128)})) conditional(s32[]{:T(128)} %convert_element_type.233, (f32[1,4,256]{2,1,0:T(4,128)S(1)}, f32[1,4,256]{2,1,0:T(4,128)S(1)}, f32[256,1,4,128]{0,3,2,1:T(8,128)}) %tuple.101, (pred[256,288]{0,1:T(8,128)(4,1)S(1)}, ...), branch_computations={%region_27.27_spmd, %region_28.30_spmd} | conditional | flops 153914368 | bytes 9773148 | solution.py:126
  163.7 3.7 %conditional.5 = ((f32[1,4,256]{2,1,0:T(4,128)S(1)}, f32[1,4,256]{2,1,0:T(4,128)S(1)}, f32[256,1,4,128]{0,3,2,1:T(8,128)})) conditional(s32[]{:T(128)} %convert_element_type.233, (f32[1,4,256]{2,1,0:T(4,128)S(1)}, f32[1,4,256]{2,1,0:T(4,128)S(1)}, f32[256,1,4,128]{0,3,2,1:T(8,128)}) %tuple.101, (pred[256,288]{0,1:T(8,128)(4,1)S(1)}, ...), branch_computations={%region_27.27_spmd, %region_28.30_spmd} | conditional | flops 153914368 | bytes 9773148 | solution.py:126
  169.7 3.7 %conditional.5 = ((f32[1,4,256]{2,1,0:T(4,128)S(1)}, f32[1,4,256]{2,1,0:T(4,128)S(1)}, f32[256,1,4,128]{0,3,2,1:T(8,128)})) conditional(s32[]{:T(128)} %convert_element_type.233, (f32[1,4,256]{2,1,0:T(4,128)S(1)}, f32[1,4,256]{2,1,0:T(4,128)S(1)}, f32[256,1,4,128]{0,3,2,1:T(8,128)}) %tuple.101, (pred[256,288]{0,1:T(8,128)(4,1)S(1)}, ...), branch_computations={%region_27.27_spmd, %region_28.30_spmd} | conditional | flops 153914368 | bytes 9773148 | solution.py:126
  175.6 3.7 %conditional.5 = ((f32[1,4,256]{2,1,0:T(4,128)S(1)}, f32[1,4,256]{2,1,0:T(4,128)S(1)}, f32[256,1,4,128]{0,3,2,1:T(8,128)})) conditional(s32[]{:T(128)} %convert_element_type.233, (f32[1,4,256]{2,1,0:T(4,128)S(1)}, f32[1,4,256]{2,1,0:T(4,128)S(1)}, f32[256,1,4,128]{0,3,2,1:T(8,128)}) %tuple.101, (pred[256,288]{0,1:T(8,128)(4,1)S(1)}, ...), branch_computations={%region_27.27_spmd, %region_28.30_spmd} | conditional | flops 153914368 | bytes 9773148 | solution.py:126
  181.6 3.7 %conditional.5 = ((f32[1,4,256]{2,1,0:T(4,128)S(1)}, f32[1,4,256]{2,1,0:T(4,128)S(1)}, f32[256,1,4,128]{0,3,2,1:T(8,128)})) conditional(s32[]{:T(128)} %convert_element_type.233, (f32[1,4,256]{2,1,0:T(4,128)S(1)}, f32[1,4,256]{2,1,0:T(4,128)S(1)}, f32[256,1,4,128]{0,3,2,1:T(8,128)}) %tuple.101, (pred[256,288]{0,1:T(8,128)(4,1)S(1)}, ...), branch_computations={%region_27.27_spmd, %region_28.30_spmd} | conditional | flops 153914368 | bytes 9773148 | solution.py:126
  187.5 3.7 %conditional.5 = ((f32[1,4,256]{2,1,0:T(4,128)S(1)}, f32[1,4,256]{2,1,0:T(4,128)S(1)}, f32[256,1,4,128]{0,3,2,1:T(8,128)})) conditional(s32[]{:T(128)} %convert_element_type.233, (f32[1,4,256]{2,1,0:T(4,128)S(1)}, f32[1,4,256]{2,1,0:T(4,128)S(1)}, f32[256,1,4,128]{0,3,2,1:T(8,128)}) %tuple.101, (pred[256,288]{0,1:T(8,128)(4,1)S(1)}, ...), branch_computations={%region_27.27_spmd, %region_28.30_spmd} | conditional | flops 153914368 | bytes 9773148 | solution.py:126
  193.5 3.7 %conditional.5 = ((f32[1,4,256]{2,1,0:T(4,128)S(1)}, f32[1,4,256]{2,1,0:T(4,128)S(1)}, f32[256,1,4,128]{0,3,2,1:T(8,128)})) conditional(s32[]{:T(128)} %convert_element_type.233, (f32[1,4,256]{2,1,0:T(4,128)S(1)}, f32[1,4,256]{2,1,0:T(4,128)S(1)}, f32[256,1,4,128]{0,3,2,1:T(8,128)}) %tuple.101, (pred[256,288]{0,1:T(8,128)(4,1)S(1)}, ...), branch_computations={%region_27.27_spmd, %region_28.30_spmd} | conditional | flops 153914368 | bytes 9773148 | solution.py:126
  198.3 3.8 %convolution_convert_fusion.1 = bf16[256,2560]{1,0:T(8,128)(2,1)} fusion(bf16[256,512]{0,1:T(8,128)(2,1)S(1)} %bitcast.148, bf16[512,2560]{1,0:T(8,128)(2,1)} %param.50), kind=kOutput, calls=%fused_computation.57 | convolution fusion | flops 671744000 | bytes 4194304 | tf_op jit(solution)/shard_map/dot_general | solution.py:156
  204.2 103.9 %all-reduce.9.cloned.1.call-done = (bf16[256,2560]{1,0:T(8,128)(2,1)}, bf16[256,2560]{1,0:T(8,128)(2,1)}) async-done(((bf16[256,2560]{1,0:T(8,128)(2,1)}, bf16[256,2560]{1,0:T(8,128)(2,1)}), (bf16[256,2560]{1,0:T(8,128)(2,1)}, bf16[256,2560]{1,0:T(8,128)(2,1)})) %all-reduce.9.cloned.1.call-update) | async-done | bytes 2621456 | tf_op jit(solution)/shard_map/psum | solution.py:267
  308.2 2.4 multiply_reduce_fusion
  312.4 2.1 fusion.72
  314.5 2.1 fusion.73
  316.6 9.6 %all-reduce.5 = (f32[256]{0:T(256)S(1)}, f32[256]{0:T(256)S(1)}) all-reduce(f32[256]{0:T(256)S(1)} %get-tuple-element.340, f32[256]{0:T(256)S(1)} %get-tuple-element.342), channel_id=1, replica_groups=mesh['seq'=8,'vocab'=4] {'vocab'}, use_global_device_ids=true, to_apply=%region_37.38 | all-reduce | flops 512 | bytes 4096 | tf_op jit(solution)/shard_map/pmax | solution.py:282
  328.0 9.3 %all-reduce.4 = (f32[256]{0:T(256)S(1)}, f32[256]{0:T(256)S(1)}, f32[256]{0:T(256)S(1)}, f32[256]{0:T(256)S(1)}) all-reduce(f32[256]{0:T(256)S(1)} %get-tuple-element.332, f32[256]{0:T(256)S(1)} %get-tuple-element.333, f32[256]{0:T(256)S(1)} %get-tuple-element.239, ...), channel_id=1, replica_groups=mesh['seq'=8,'vocab'=4] {'vocab'}, use_global_device_ids=true, to_apply=%region_35.36 | all-reduce | flops 1024 | bytes 8192 | tf_op jit(solution)/shard_map/psum | solution.py:285
  338.0 12.3 %psum.55 = f32[4]{0:T(128)} all-reduce(f32[4]{0:T(128)S(1)} %select_reduce_fusion.2), channel_id=1, replica_groups=mesh['seq'=8,'vocab'=4] {'seq'}, use_global_device_ids=true, to_apply=%region_43.44 | all-reduce | flops 4 | bytes 32 | tf_op jit(solution)/shard_map/psum | solution.py:293
  (383 shorter events, 143.4 us)
Async XLA Ops:
  7.2 304.0 %copy-start = (bf16[2560,640]{1,0:T(8,128)(2,1)S(1)}, bf16[2560,640]{1,0:T(8,128)(2,1)}, u32[]{:S(2)}) copy-start(bf16[2560,640]{1,0:T(8,128)(2,1)} %param.63) | copy-start | bytes 9830404
  7.2 6.8 %copy-start.40 = (f32[2560]{0:T(1024)S(1)}, f32[2560]{0:T(1024)}, u32[]{:S(2)}) copy-start(f32[2560]{0:T(1024)} %param.44) | copy-start | bytes 30724
  7.2 92.2 %all-gather.3.cloned.1.call-start = ((), (), s32[]{:S(2)}) async-start(), calls=%async_computation | async-start | bytes 1327104 | tf_op jit(solution)/shard_map/all_gather | solution.py:247
  9.5 4.5 %copy-start.8 = (bf16[256,2560]{1,0:T(8,128)(2,1)S(1)}, bf16[256,2560]{1,0:T(8,128)(2,1)}, u32[]{:S(2)}) copy-start(bf16[256,2560]{1,0:T(8,128)(2,1)} %param.37) | copy-start | bytes 3932164
  14.0 5.9 %copy-start.31 = (f32[256]{0:T(256)}, f32[256]{0:T(256)S(1)}, u32[]{:S(2)}) copy-start(f32[256]{0:T(256)S(1)} %add_rsqrt_fusion.7) | copy-start | bytes 3076
  14.0 2.7 copy-start.6
  19.9 2.8 copy-start.23
  19.9 3.5 copy-start.24
  26.2 6.0 %copy-start.32 = (f32[256]{0:T(256)S(1)}, f32[256]{0:T(256)}, u32[]{:S(2)}) copy-start(f32[256]{0:T(256)} %copy-done.31) | copy-start | bytes 3076
  29.6 119.1 %all-gather.5.cloned.1.call-start = ((), (), s32[]{:S(2)}) async-start(), calls=%async_computation.1 | async-start | bytes 1327104 | tf_op jit(solution)/shard_map/all_gather | solution.py:257
  30.5 277.7 %all-reduce.9.cloned.1.call-start = ((), (), s32[]{:S(2)}) async-start(), calls=%async_computation.2 | async-start | bytes 5242880 | tf_op jit(solution)/shard_map/psum | solution.py:267
  36.0 4.1 %copy-start.34 = (f32[256]{0:T(256)S(1)}, f32[256]{0:T(256)}, u32[]{:S(2)}) copy-start(f32[256]{0:T(256)} %copy-done.33) | copy-start | bytes 3076
  36.0 4.1 %copy-start.42 = (f32[2560]{0:T(1024)S(1)}, f32[2560]{0:T(1024)}, u32[]{:S(2)}) copy-start(f32[2560]{0:T(1024)} %param.55) | copy-start | bytes 30724
  43.9 4.6 %copy-start.17 = (f32[256,128]{0,1:T(8,128)S(1)}, f32[256,128]{0,1:T(8,128)}, u32[]{:S(2)}) copy-start(f32[256,128]{0,1:T(8,128)} %get-tuple-element.344) | copy-start | bytes 393220
  108.6 2.3 copy-start.4
  114.7 2.3 copy-start.4
  126.8 2.3 copy-start.4
  132.9 2.3 copy-start.4
  145.0 2.3 copy-start.4
  157.8 2.3 copy-start.1
  163.7 2.3 copy-start.1
  169.7 2.3 copy-start.1
  187.5 2.3 copy-start.1
  193.5 2.3 copy-start.1
  198.3 3.8 %copy-start.3 = (f32[256,1,4,128]{0,3,2,1:T(8,128)S(1)}, f32[256,1,4,128]{0,3,2,1:T(8,128)}, u32[]{:S(2)}) copy-start(f32[256,1,4,128]{0,3,2,1:T(8,128)} %get-tuple-element.214) | copy-start | bytes 1572868
  198.3 3.9 %copy-start.11 = (bf16[512,2560]{1,0:T(8,128)(2,1)S(1)}, bf16[512,2560]{1,0:T(8,128)(2,1)}, u32[]{:S(2)}) copy-start(bf16[512,2560]{1,0:T(8,128)(2,1)} %param.61) | copy-start | bytes 7864324
  204.2 107.0 %copy-start.43 = (f32[2560]{0:T(1024)S(1)}, f32[2560]{0:T(1024)}, u32[]{:S(2)}) copy-start(f32[2560]{0:T(1024)} %param.62) | copy-start | bytes 30724
  308.2 2.4 copy-start.9
  308.2 2.5 copy-start.14
  314.5 11.7 %copy-start.35 = (s32[256]{0:T(256)S(1)}, s32[256]{0:T(256)}, u32[]{:S(2)}) copy-start(s32[256]{0:T(256)} %param.39) | copy-start | bytes 3076
  316.6 20.6 %copy-start.25 = (s32[256]{0:T(256)S(1)}, s32[256]{0:T(256)}, u32[]{:S(2)}) copy-start(s32[256]{0:T(256)} %get-tuple-element.243) | copy-start | bytes 3076
  316.6 21.2 %copy-start.26 = (s32[256]{0:T(256)S(1)}, s32[256]{0:T(256)}, u32[]{:S(2)}) copy-start(s32[256]{0:T(256)} %get-tuple-element.242) | copy-start | bytes 3076
  (44 other events, 59.4 us)
Sparse Core Ops, SparseCore 0:
  29.7 26.7 all-gather.2
  58.4 24.1 all-gather.4
  204.3 103.7 all-reduce.8
where the time goes:
time: 360 us; the launch traced here: 357 us
  waiting for transfers between devices  104 us (29%)
  local copies, waits for them, and re-layouts  65.4 us (18%)
  blocking collectives  58.2 us (16%)
  matrix products  52.3 us (15%)
  other arithmetic  49.7 us (14%)
  between operations  14.9 us (4%)
  loops' own time  12.1 us (3%)
    psum x1, waiting for transfers between devices, local(): lax.psum(reference_part.astype(jnp.bfloat16), 'vocab').astype(jnp.float32)  104 us
    unnamed x1, blocking collectives  27 us
    dot_general x16, matrix products, update_state(): jnp.einsum('qkgd,skd->kgqs', query_rows, key_part, preferred_element_type...  20.8 us
    squeeze x16, local copies, waits for them, and re-layouts, fold_pieces(): return lax.scan(scan_step, states, split_pieces)[0]  15.7 us
    reduce_or x16, other arithmetic, attend(): return lax.cond(jnp.any(visible), compute, unchanged, states)  13.3 us
    psum x1, blocking collectives, local(): rollout_mean = lax.psum(partial_sums, 'seq')  12.3 us
    dynamic_slice x16, local copies, waits for them, and re-layouts, fold_pieces(): return lax.scan(scan_step, states, split_pieces)[0]  12 us
    another operation x2, loops' own time, fold_pieces(): return lax.scan(scan_step, states, split_pieces)[0]  11 us
  transfers between devices with their start and end apart: 3, of which 1 were waited for; matrix products, arithmetic and copies ran while one was open for 22% of the time, Pallas kernels for 0%

commit v1 on v0

v1 whole, which is shorter than its diff:
```python
import functools

import jax
import jax.numpy as jnp
from jax import lax
from jax.experimental import pallas as pl
from jax.experimental.pallas import tpu as pltpu
from jax.sharding import PartitionSpec as P

HD = 128
BLOCK = 128
EPSILON = 1e-06
ROPE_BASE = 1000000.0
NEGATIVE_FILL = -1e30
CHUNK = 64
MESH = pl.DeviceIdType.MESH
F32 = jnp.float32
BF16 = jnp.bfloat16


def dot(a, b):
    return jnp.dot(a, b, preferred_element_type=F32)


def dot_t(a, b):
    return lax.dot_general(a, b, (((1,), (1,)), ((), ())), preferred_element_type=F32)


def kernel(
    n_seq,
    rolls,
    col_ref,
    row_ref,
    cos_ref,
    sin_ref,
    prompt_ref,
    hid_p,
    hid_r,
    ing_p,
    ing_r,
    qg_p,
    qg_r,
    kg_p,
    kg_r,
    fg_p,
    fg_r,
    wq_p,
    wq_r,
    wk_p,
    wk_r,
    wv_p,
    wv_r,
    wo_p,
    wo_r,
    hd_p,
    hd_r,
    diff_ref,
    mean_ref,
    wq,
    wk,
    wv,
    wo,
    hd,
    hid,
    fgain,
    normed,
    query,
    kv,
    pbuf,
    codes,
    bias,
    mx_s,
    sum_s,
    acc,
    attended,
    part,
    inbuf,
    xs,
    xr,
    own,
    fin,
    stat,
    sbuf,
    rbuf,
    w_sem,
    kv_s,
    kv_r,
    p_s,
    p_r,
    c_s,
    c_r,
    in_s,
    in_r,
    x_s,
    x_r,
    f_s,
    f_r,
    e_s,
    e_r,
    st_s,
    st_r,
    ro_s,
    ro_r,
):
    seq = lax.axis_index("seq")
    voc = lax.axis_index("vocab")
    rows = hid.shape[1]
    width = hid.shape[2]
    heads = query.shape[1]
    n_chips = n_seq // 2
    n_voc = 4
    chip = seq // 2
    core = seq % 2
    sibling = chip * 2 + (1 - core)
    chunks = rows // CHUNK
    total = 2 * chunks
    half = CHUNK // 2
    words = hd.shape[2]
    scale = HD ** (-0.5)

    def remote(src, dst, send, recv, s, v):
        return pltpu.make_async_remote_copy(
            src_ref=src, dst_ref=dst, send_sem=send, recv_sem=recv, device_id=(s, v), device_id_type=MESH
        )

    loads = []
    order = (
        (hid_p, hid, 0), (wk_p, wk, 0), (wv_p, wv, 0), (wq_p, wq, 0),
        (hid_r, hid, 1), (wk_r, wk, 1), (wv_r, wv, 1), (wq_r, wq, 1),
        (wo_p, wo, 0), (wo_r, wo, 1), (hd_p, hd, 0), (hd_r, hd, 1),
    )
    for i, (src, dst, m) in enumerate(order):
        copy = pltpu.make_async_copy(src, dst.at[m], w_sem.at[i])
        copy.start()
        loads.append(copy)

    barrier = pltpu.get_barrier_semaphore()

    def greet_seq(j, carry):
        pl.semaphore_signal(barrier, inc=1, device_id=((seq + j) % n_seq, voc), device_id_type=MESH)
        return carry

    def greet_voc(j, carry):
        pl.semaphore_signal(barrier, inc=1, device_id=(seq, (voc + j) % n_voc), device_id_type=MESH)
        return carry

    lax.fori_loop(1, n_seq, greet_seq, 0)
    lax.fori_loop(1, n_voc, greet_voc, 0)
    fgain[0] = fg_p[...]
    fgain[1] = fg_r[...]
    stat[...] = jnp.zeros_like(stat)
    pbuf[seq] = prompt_ref[...]
    codes[seq] = row_ref[...]
    pl.semaphore_wait(barrier, n_seq - 1 + n_voc - 1)

    def prompt_copy(j):
        peer = (seq + j) % n_seq
        return remote(prompt_ref, pbuf.at[seq], p_s.at[j], p_r.at[seq], peer, voc)

    def code_copy(j):
        peer = (seq + j) % n_seq
        return remote(row_ref, codes.at[seq], c_s.at[j], c_r.at[seq], peer, voc)

    def send_small(j, carry):
        prompt_copy(j).start()
        code_copy(j).start()
        return carry

    lax.fori_loop(1, n_seq, send_small, 0)

    def kv_copy(m, src, dst_seq, slot):
        return remote(kv.at[m, src], kv.at[m, src], kv_s.at[m, slot], kv_r.at[m, src], dst_seq, voc)

    def turn(values, gain):
        values = values * lax.rsqrt(jnp.mean(values * values, axis=-1, keepdims=True) + EPSILON) * gain
        return (values * cos_ref[...] + pltpu.roll(values, HD // 2, axis=1) * sin_ref[...]).astype(BF16)

    for m in range(2):
        ing, qg, kg = ((ing_p, qg_p, kg_p), (ing_r, qg_r, kg_r))[m]
        loads[4 * m].wait()

        def norm_rows(i, carry, m=m, ing=ing):
            here = pl.ds(pl.multiple_of(i * 32, 32), 32)
            values = hid[m, here, :].astype(F32)
            inv = lax.rsqrt(jnp.mean(values * values, axis=-1, keepdims=True) + EPSILON)
            normed[here, :] = (values * inv * ing[...]).astype(BF16)
            return carry

        lax.fori_loop(0, rows // 32, norm_rows, 0)
        loads[4 * m + 1].wait()
        loads[4 * m + 2].wait()
        key_rows = turn(dot(normed[...], wk[m]), kg[...])
        kv[m, seq, :, 0:HD] = key_rows
        kv[m, seq, :, HD : 2 * HD] = dot(normed[...], wv[m]).astype(BF16)
        kv_copy(m, seq, sibling, 0).start()

        def send_kv(j, carry, m=m):
            kv_copy(m, seq, ((chip + j) % n_chips) * 2 + core, j).start()
            return carry

        lax.fori_loop(1, n_chips, send_kv, 0)
        loads[4 * m + 3].wait()
        for h in range(0, heads, 2):
            both = dot(normed[...], wq[m, :, h * HD : (h + 2) * HD])
            query[m, h] = turn(both[:, :HD], qg[...])
            query[m, h + 1] = turn(both[:, HD:], qg[...])

    def wait_small(j, carry):
        src = (seq + n_seq - j) % n_seq
        remote(prompt_ref, pbuf.at[src], p_s.at[j], p_r.at[src], src, voc).wait_recv()
        remote(row_ref, codes.at[src], c_s.at[j], c_r.at[src], src, voc).wait_recv()
        prompt_copy(j).wait_send()
        code_copy(j).wait_send()
        return carry

    lax.fori_loop(1, n_seq, wait_small, 0)
    loads[8].wait()
    loads[9].wait()

    first = col_ref[:, 0:1]
    index = col_ref[:, 1:2]
    prompt = col_ref[:, 2:3]
    prompt_rows = pbuf.shape[2]
    per_prompt = prompt_rows // 4

    def tile(m, src):
        code = codes[src][0:1, :]
        bias[...] = jnp.where((code >= first) & (code <= index), 0.0, NEGATIVE_FILL)

        def head_step(h, carry):
            scores = dot_t(query[m, h], kv[m, src, :, 0:HD]) * scale + bias[...]
            old = mx_s[h]
            new = jnp.maximum(old, jnp.max(scores, axis=-1, keepdims=True))
            weights = jnp.exp(scores - new[:, 0:1])
            factor = jnp.exp(old - new)
            mx_s[h] = new
            sum_s[h] = sum_s[h] * factor + jnp.sum(weights, axis=-1, keepdims=True)
            acc[h] = acc[h] * factor + dot(weights.astype(BF16), kv[m, src, :, HD : 2 * HD])
            return carry

        lax.fori_loop(0, heads, head_step, 0, unroll=True)

    is_end = (voc == 0) | (voc == n_voc - 1)
    middle = 1 + voc // 2
    end = (voc // 2) * 3
    other = 3 - voc

    def rows_of(k, off, count):
        return pl.ds(pl.multiple_of((k % chunks) * CHUNK + off, half), count)

    def partial_chunk(k, store):
        m = k // chunks
        values = attended[m, rows_of(k, 0, CHUNK), :]
        for c in range(0, width, 512):
            store(c, dot(values, wo[m, :, c : c + 512]))

    def in_copy(k):
        m, here = k // chunks, rows_of(k, 0, CHUNK)
        return remote(part.at[m, here, :], inbuf.at[m, here, :], in_s.at[k], in_r.at[k], seq, middle)

    def attend(m, carry):
        prompts = pbuf[:, m].reshape(n_seq * prompt_rows, 2 * HD)
        owner = (lax.broadcasted_iota(jnp.int32, (1, n_seq * prompt_rows), 1) % prompt_rows) // per_prompt
        cover = owner == prompt
        for h in range(heads):
            scores = jnp.where(cover, dot_t(query[m, h], prompts[:, :HD]) * scale, NEGATIVE_FILL)
            top = jnp.max(scores, axis=-1, keepdims=True)
            weights = jnp.exp(scores - top)
            mx_s[h] = jnp.broadcast_to(top, (rows, HD))
            sum_s[h] = jnp.broadcast_to(jnp.sum(weights, axis=-1, keepdims=True), (rows, HD))
            acc[h] = dot(weights.astype(BF16), prompts[:, HD:])

        tile(m, seq)
        kv_copy(m, sibling, sibling, 0).wait_recv()
        tile(m, sibling)

        def chip_step(j, inner):
            src_chip = (chip + n_chips - j) % n_chips
            src = src_chip * 2 + core
            kv_copy(m, src, sibling, 0).wait_recv()
            kv_copy(m, src, sibling, n_chips + j).start()
            tile(m, src)
            src_sib = src_chip * 2 + (1 - core)
            kv_copy(m, src_sib, sibling, 0).wait_recv()
            tile(m, src_sib)
            return inner

        lax.fori_loop(1, n_chips, chip_step, 0)
        for h in range(heads):
            attended[m, :, h * HD : (h + 1) * HD] = (acc[h] / sum_s[h]).astype(BF16)

        @pl.when(is_end)
        def _():
            def send_chunk(i, inner):
                k = m * chunks + i

                def store(c, value):
                    part[m, rows_of(k, 0, CHUNK), c : c + 512] = value.astype(BF16)

                partial_chunk(k, store)
                in_copy(k).start()
                return inner

            lax.fori_loop(0, chunks, send_chunk, 0)

        return carry

    lax.fori_loop(0, 2, attend, 0)
    loads[10].wait()
    loads[11].wait()

    lanes = lax.broadcasted_iota(jnp.int32, (CHUNK, 128), 1)

    def head_chunk(k):
        m, here = k // chunks, rows_of(k, 0, CHUNK)
        logits = dot(fin[m, here, :], hd[m])
        top = jnp.max(logits, axis=-1, keepdims=True)
        mass = jnp.sum(jnp.exp(logits - top), axis=-1, keepdims=True)
        word = voc * words + lax.broadcasted_iota(jnp.int32, (CHUNK, words), 1)
        target = col_ref[here, 3:4]
        hit = jnp.sum(jnp.where(word == target, logits, 0.0), axis=-1, keepdims=True)
        old = stat[here, :]
        old = jnp.where(lanes == 3 * m, top, old)
        old = jnp.where(lanes == 3 * m + 1, mass, old)
        stat[here, :] = jnp.where(lanes == 3 * m + 2, hit, old)

    mine = (voc - 1) * half
    theirs = half - mine

    def x_copy(k):
        return remote(xs.at[k], xr.at[k], x_s.at[k], x_r.at[k], seq, other)

    def f_copy(k, off):
        ref = fin.at[k // chunks, rows_of(k, off, half), :]
        return remote(ref, ref, f_s.at[k], f_r.at[k], seq, other)

    def e_copy(k, off, which):
        ref = fin.at[k // chunks, rows_of(k, off, half), :]
        return remote(ref, ref, e_s.at[2 * k + which], e_r.at[2 * k + which], seq, end)

    @pl.when(is_end)
    def _():
        def step(k, carry):
            first_off = (middle - 1) * half
            for which, off in ((0, first_off), (1, half - first_off)):
                ref = fin.at[k // chunks, rows_of(k, off, half), :]
                remote(ref, ref, e_s.at[2 * k + which], e_r.at[2 * k + which], seq, middle).wait_recv()
            head_chunk(k)
            in_copy(k).wait_send()
            return carry

        lax.fori_loop(0, total, step, 0)

    @pl.when(jnp.logical_not(is_end))
    def _():
        def pass_on(k):
            f_copy(k, theirs).wait_recv()
            e_copy(k, theirs, 1).start()
            head_chunk(k)

        def step(k, carry):
            m = k // chunks

            def store(c, value):
                own[:, c : c + 512] = value

            partial_chunk(k, store)
            pltpu.make_async_remote_copy(
                src_ref=part.at[m, rows_of(k, 0, CHUNK), :],
                dst_ref=inbuf.at[m, rows_of(k, 0, CHUNK), :],
                send_sem=in_s.at[k],
                recv_sem=in_r.at[k],
                device_id=(seq, end),
                device_id_type=MESH,
            ).wait_recv()
            away = pl.ds(pl.multiple_of(theirs, half), half)
            xs[k] = (own[away, :] + inbuf[m, rows_of(k, theirs, half), :].astype(F32)).astype(BF16)
            x_copy(k).start()

            @pl.when(k > 0)
            def _():
                pass_on(k - 1)

            home = pl.ds(pl.multiple_of(mine, half), half)
            here = rows_of(k, mine, half)
            mixed = own[home, :] + inbuf[m, here, :].astype(F32)
            x_copy(k).wait_recv()
            values = hid[m, here, :].astype(F32) + (mixed + xr[k].astype(F32))
            inv = lax.rsqrt(jnp.mean(values * values, axis=-1, keepdims=True) + EPSILON)
            fin[m, here, :] = (values * inv * fgain[m]).astype(BF16)
            f_copy(k, mine).start()
            e_copy(k, mine, 0).start()
            return carry

        lax.fori_loop(0, total, step, 0)
        pass_on(total - 1)

        def drain(k, carry):
            x_copy(k).wait_send()
            f_copy(k, mine).wait_send()
            e_copy(k, mine, 0).wait_send()
            e_copy(k, theirs, 1).wait_send()
            return carry

        lax.fori_loop(0, total, drain, 0)

    sbuf[voc] = jnp.transpose(stat[...])[0:8, :]

    def stat_copy(j):
        return remote(sbuf.at[voc], sbuf.at[voc], st_s.at[j], st_r.at[voc], seq, (voc + j) % n_voc)

    for j in range(1, n_voc):
        stat_copy(j).start()
    for m in range(2):
        def drain_kv(j, carry, m=m):
            kv_copy(m, seq, sibling, j).wait_send()
            return carry

        lax.fori_loop(0, n_chips, drain_kv, 0)
        lax.fori_loop(n_chips + 1, 2 * n_chips, drain_kv, 0)
    for j in range(1, n_voc):
        src = (voc + n_voc - j) % n_voc
        remote(sbuf.at[src], sbuf.at[src], st_s.at[j], st_r.at[src], seq, src).wait_recv()
    parts = [sbuf[v] for v in range(n_voc)]

    def score(m):
        top = functools.reduce(jnp.maximum, [p[3 * m : 3 * m + 1] for p in parts])
        mass = sum(p[3 * m + 1 : 3 * m + 2] * jnp.exp(p[3 * m : 3 * m + 1] - top) for p in parts)
        hit = sum(p[3 * m + 2 : 3 * m + 3] for p in parts)
        return hit - (top + jnp.log(mass))

    diff = score(0) - score(1)
    diff_ref[...] = diff
    per_token = diff / row_ref[2:3, :].astype(F32)
    slot = row_ref[1:2, :]
    lane = lax.broadcasted_iota(jnp.int32, (8, 128), 1)
    block = jnp.zeros((8, 128), F32)
    for r in range(rolls):
        piece = jnp.sum(jnp.where(slot == r, per_token, 0.0), axis=1, keepdims=True)
        block = jnp.where(lane == r, piece, block)
    rbuf[seq] = block

    def roll_copy(j):
        return remote(rbuf.at[seq], rbuf.at[seq], ro_s.at[j], ro_r.at[seq], (seq + j) % n_seq, voc)

    def start_roll(j, carry):
        roll_copy(j).start()
        return carry

    def wait_roll(j, carry):
        src = (seq + n_seq - j) % n_seq
        remote(rbuf.at[src], rbuf.at[src], ro_s.at[j], ro_r.at[src], src, voc).wait_recv()
        return carry

    def drain_roll(j, carry):
        roll_copy(j).wait_send()
        return carry

    lax.fori_loop(1, n_seq, start_roll, 0)
    lax.fori_loop(1, n_seq, wait_roll, 0)
    mean_ref[...] = jnp.sum(rbuf[...], axis=0)
    lax.fori_loop(1, n_seq, drain_roll, 0)
    for j in range(1, n_voc):
        stat_copy(j).wait_send()


def local(
    policy_hidden,
    reference_hidden,
    targets,
    lengths,
    block_source,
    rollout_prompt,
    rollout_slot,
    policy_input_gain,
    policy_query_weight,
    policy_key_weight,
    policy_value_weight,
    policy_query_gain,
    policy_key_gain,
    policy_out_weight,
    policy_final_gain,
    policy_head,
    policy_prompt_keys,
    policy_prompt_values,
    reference_input_gain,
    reference_query_weight,
    reference_key_weight,
    reference_value_weight,
    reference_query_gain,
    reference_key_gain,
    reference_out_weight,
    reference_final_gain,
    reference_head,
    reference_prompt_keys,
    reference_prompt_values,
):
    n_seq = lax.axis_size("seq")
    rows, width = policy_hidden.shape
    rolls = lengths.shape[0]
    heads = policy_query_weight.shape[1] // HD
    words = policy_head.shape[1]
    chunks = rows // CHUNK
    total = 2 * chunks
    prompt_count, prefix_local = policy_prompt_keys.shape[:2]
    prompt_rows = prompt_count * prefix_local

    slot_ids = jnp.arange(rows, dtype=jnp.int32)
    packed = jnp.repeat(block_source, BLOCK) * BLOCK + slot_ids % BLOCK
    ends = jnp.cumsum(lengths)
    rollout = jnp.sum((packed[:, None] >= ends[None, :]).astype(jnp.int32), axis=1)
    member = rollout[:, None] == jnp.arange(rolls, dtype=jnp.int32)[None, :]

    def lookup(table):
        return jnp.sum(jnp.where(member, table[None, :], 0), axis=1)

    first = lookup(ends - lengths)
    zero = jnp.zeros_like(packed)
    col = jnp.stack([first, packed, lookup(rollout_prompt), targets], axis=1)
    col = jnp.pad(col, ((0, 0), (0, 124)))
    row = jnp.stack([packed, lookup(rollout_slot), lookup(lengths), zero, zero, zero, zero, zero], axis=0)
    frequency = ROPE_BASE ** (-2.0 * jnp.arange(HD // 2, dtype=F32) / HD)
    place = packed - first + prefix_local * n_seq
    angles = place.astype(F32)[:, None] * frequency[None, :]
    cosine, sine = jnp.cos(angles), jnp.sin(angles)
    cosine = jnp.concatenate([cosine, cosine], axis=1)
    sine = jnp.concatenate([-sine, sine], axis=1)

    def both(keys, values):
        return jnp.concatenate([keys.reshape(prompt_rows, HD), values.reshape(prompt_rows, HD)], axis=1)

    prompts = jnp.stack(
        [both(policy_prompt_keys, policy_prompt_values), both(reference_prompt_keys, reference_prompt_values)]
    )
    vmem = pl.BlockSpec(memory_space=pltpu.VMEM)
    hbm = pl.BlockSpec(memory_space=pl.ANY)
    dma = pltpu.SemaphoreType.DMA
    n_chips = n_seq // 2
    diff, mean = pl.pallas_call(
        functools.partial(kernel, n_seq, rolls),
        out_shape=(
            jax.ShapeDtypeStruct((1, rows), F32),
            jax.ShapeDtypeStruct((8, 128), F32),
        ),
        in_specs=[vmem] * 5 + [hbm] * 2 + [vmem] * 8 + [hbm] * 10,
        out_specs=(vmem, vmem),
        scratch_shapes=[
            pltpu.VMEM((2, width, heads * HD), BF16),
            pltpu.VMEM((2, width, HD), BF16),
            pltpu.VMEM((2, width, HD), BF16),
            pltpu.VMEM((2, heads * HD, width), BF16),
            pltpu.VMEM((2, width, words), BF16),
            pltpu.VMEM((2, rows, width), BF16),
            pltpu.VMEM((2, 1, width), F32),
            pltpu.VMEM((rows, width), BF16),
            pltpu.VMEM((2, heads, rows, HD), BF16),
            pltpu.VMEM((2, n_seq, rows, 2 * HD), BF16),
            pltpu.VMEM((n_seq, 2, prompt_rows, 2 * HD), BF16),
            pltpu.VMEM((n_seq, 8, rows), jnp.int32),
            pltpu.VMEM((rows, rows), F32),
            pltpu.VMEM((heads, rows, HD), F32),
            pltpu.VMEM((heads, rows, HD), F32),
            pltpu.VMEM((heads, rows, HD), F32),
            pltpu.VMEM((2, rows, heads * HD), BF16),
            pltpu.VMEM((2, rows, width), BF16),
            pltpu.VMEM((2, rows, width), BF16),
            pltpu.VMEM((total, CHUNK // 2, width), BF16),
            pltpu.VMEM((total, CHUNK // 2, width), BF16),
            pltpu.VMEM((CHUNK, width), F32),
            pltpu.VMEM((2, rows, width), BF16),
            pltpu.VMEM((rows, 128), F32),
            pltpu.VMEM((4, 8, rows), F32),
            pltpu.VMEM((n_seq, 8, 128), F32),
            dma((12,)),
            dma((2, n_seq)),
            dma((2, n_seq)),
            dma((n_seq,)),
            dma((n_seq,)),
            dma((n_seq,)),
            dma((n_seq,)),
            dma((total,)),
            dma((total,)),
            dma((total,)),
            dma((total,)),
            dma((total,)),
            dma((total,)),
            dma((2 * total,)),
            dma((2 * total,)),
            dma((4,)),
            dma((4,)),
            dma((n_seq,)),
            dma((n_seq,)),
        ],
        compiler_params=pltpu.CompilerParams(
            collective_id=0, has_side_effects=True, vmem_limit_bytes=60 * 1024 * 1024
        ),
    )(
        col,
        row,
        cosine,
        sine,
        prompts,
        policy_hidden,
        reference_hidden,
        policy_input_gain[None],
        reference_input_gain[None],
        policy_query_gain[None],
        reference_query_gain[None],
        policy_key_gain[None],
        reference_key_gain[None],
        policy_final_gain[None],
        reference_final_gain[None],
        policy_query_weight,
        reference_query_weight,
        policy_key_weight,
        reference_key_weight,
        policy_value_weight,
        reference_value_weight,
        policy_out_weight,
        reference_out_weight,
        policy_head,
        reference_head,
    )
    return (diff.reshape(rows), mean[0, :rolls])


def solution(mesh):
    model_specs = (
        P(),
        P(None, "vocab"),
        P(None, "vocab"),
        P(None, "vocab"),
        P(),
        P(),
        P("vocab", None),
        P(),
        P(None, "vocab"),
        P(None, "seq", "vocab"),
        P(None, "seq", "vocab"),
    )
    return jax.shard_map(
        local,
        mesh=mesh,
        in_specs=(P("seq", None), P("seq", None), P("seq"), P(), P("seq"), P(), P()) + model_specs * 2,
        out_specs=(P("seq"), P()),
        check_vma=False,
    )
```

time: 360 us -> 139 us (0.39)
  Pallas kernels: 0 us -> 122 us
  waiting for transfers between devices: 104 us -> 0 us
  blocking collectives: 58.2 us -> 0 us
  local copies, waits for them, and re-layouts: 65.4 us -> 9.13 us
  matrix products: 52.3 us -> 0 us
  other arithmetic: 49.7 us -> 6.6 us
  between operations: 14.9 us -> 0.67 us
  loops' own time: 12.1 us -> 0 us
    pallas_call x0 -> x1, Pallas kernels: none -> 122 us  [local(): pl.pallas_call(functools.partial(kernel, n_seq, rolls), out_shape=(jax.Sh...]
    psum x1 -> x0, waiting for transfers between devices: 104 us -> none  [local(): lax.psum(reference_part.astype(jnp.bfloat16), 'vocab').astype(jnp.float32)]
    dot_general x42 -> x0, matrix products: 52.3 us -> none  [the longest x16 20.8 us: update_state(): jnp.einsum('qkgd,skd->kgqs', query_rows, key_part, preferred_element_type...]
    unnamed x1 -> x0, blocking collectives: 27 us -> none
    psum x2 -> x0, blocking collectives: 21.6 us -> none  [the longest x1 12.3 us: local(): rollout_mean = lax.psum(partial_sums, 'seq')]
    reduce_sum x26 -> x2, other arithmetic: 16 us -> 0.86 us  [the longest x1 0.77 us: lookup(): return jnp.sum(jnp.where(member, table[None, :], 0), axis=1)]
    squeeze x16 -> x1, local copies, waits for them, and re-layouts: 15.7 us -> 1.19 us  [local(): return (diff.reshape(rows), mean[0, :rolls])]
    reshape x10 -> x0, local copies, waits for them, and re-layouts: 13.7 us -> none  [the longest x4 8.11 us: project(): jnp.dot(normed, query_weight, preferred_element_type=jnp.float32)]
  transfers between devices with their start and end apart: 3 -> 0, of which waited for: 1 -> 0; matrix products, arithmetic and copies ran while one was open for 22% -> 0% of each run, Pallas kernels for 0% -> 0%
where the time goes in v1:
time: 139 us
  Pallas kernels  122 us (88%)
  local copies, waits for them, and re-layouts  9.13 us (7%)
  other arithmetic  6.6 us (5%)
    pallas_call x1, Pallas kernels, local(): pl.pallas_call(functools.partial(kernel, n_seq, rolls), out_shape=(jax.Sh...  122 us

profile of v1, /device:TPU:0, one launch (start us, length us, event | category | flops | bytes accessed | tf_op | source)
XLA Modules:
  0.0 138.6 jit_solution(7324545496061017763)
XLA Ops:
  0.6 0.7 broadcast_multiply_fusion
  1.3 0.1 fusion.3
  1.4 0.8 reduce-window.8
  2.2 0.1 convert_reduce_fusion
  2.3 0.7 bitcast_subtract_fusion
  2.9 0.8 select_reduce_fusion
  3.7 0.1 add_convert_fusion
  3.8 0.5 fusion
  4.3 0.8 pad_maximum_fusion
  5.2 0.1 broadcast_in_dim.67
  5.3 0.7 pad_add_fusion
  6.0 0.1 copy.36
  6.1 0.7 pad.4.col_ref
  6.8 0.6 stack.42.row_ref
  7.4 0.8 maximum_bitcast_fusion
  8.1 0.6 pad_maximum_fusion.2.prompt_ref
  8.7 1.3 broadcast_in_dim.73.ing_p
  10.0 1.3 broadcast_in_dim.74.ing_r
  11.4 1.3 broadcast_in_dim.79.fg_p
  12.7 1.3 broadcast_in_dim.80.fg_r
  14.0 122.1 %shard_map.284 = (f32[1,256]{1,0:T(1,128)}, f32[8,128]{1,0:T(8,128)}) custom-call(s32[256,128]{1,0:T(8,128)} %pad.4.col_ref, s32[8,256]{1,0:T(8,128)} %stack.42.row_ref, f32[256,128]{1,0:T(8,128)} %get-tuple-element.13.cos_ref, f32[256,128]{1,0:T(8,128)} %get-tuple-element.14.sin_ref, bf16[2,32,256]{2,1,0:T(8,128)(2,1)} %pad_maximum_fusion.2.prompt_ref, ...), custom_call_target="tpu_custom_call" | custom-call | tf_op jit(solution)/shard_map/pallas_call | solution.py:539
  136.1 1.2 slice_bitcast_fusion
  137.3 1.2 copy.38
  (5 shorter events, 0.0 us)

commit v2 on v1

--- a/solution.py
+++ b/solution.py
@@ -2,6 +2,7 @@
 
 import jax
 import jax.numpy as jnp
+import numpy as np
 from jax import lax
 from jax.experimental import pallas as pl
 from jax.experimental.pallas import tpu as pltpu
@@ -29,11 +30,16 @@
 def kernel(
     n_seq,
     rolls,
-    col_ref,
-    row_ref,
-    cos_ref,
-    sin_ref,
-    prompt_ref,
+    lens,
+    source,
+    prompt_of,
+    slot_of,
+    tgt_ref,
+    freq_ref,
+    pk_p,
+    pv_p,
+    pk_r,
+    pv_r,
     hid_p,
     hid_r,
     ing_p,
@@ -63,21 +69,22 @@
     hd,
     hid,
     fgain,
-    normed,
     query,
     kv,
     pbuf,
     codes,
     bias,
-    mx_s,
-    sum_s,
-    acc,
+    kept,
+    col_ref,
+    cos_ref,
+    sin_ref,
+    igain,
     attended,
-    part,
     inbuf,
     xs,
     xr,
     own,
+    keep,
     fin,
     stat,
     sbuf,
@@ -146,20 +153,44 @@
 
     lax.fori_loop(1, n_seq, greet_seq, 0)
     lax.fori_loop(1, n_voc, greet_voc, 0)
-    fgain[0] = fg_p[...]
-    fgain[1] = fg_r[...]
+    fgain[0] = fg_p[...].reshape(1, width)
+    fgain[1] = fg_r[...].reshape(1, width)
+    igain[0] = ing_p[...].reshape(1, width)
+    igain[1] = ing_r[...].reshape(1, width)
     stat[...] = jnp.zeros_like(stat)
-    pbuf[seq] = prompt_ref[...]
-    codes[seq] = row_ref[...]
+    prompt_rows = pbuf.shape[2]
+    per_prompt = pk_p.shape[1]
+    for m, (keys, values) in enumerate(((pk_p, pv_p), (pk_r, pv_r))):
+        pbuf[seq, m, :, 0:HD] = keys[...].astype(F32).reshape(prompt_rows, HD).astype(BF16)
+        pbuf[seq, m, :, HD : 2 * HD] = values[...].astype(F32).reshape(prompt_rows, HD).astype(BF16)
+
+    starts = [jnp.int32(0)]
+    for r in range(rolls):
+        starts.append(starts[-1] + lens[r])
+
+    def packed_of(slot):
+        packed = slot + (source[0] * BLOCK)
+        for b in range(1, rows // BLOCK):
+            packed = jnp.where(slot >= b * BLOCK, slot + (source[b] - b) * BLOCK, packed)
+        return packed
+
+    def lookup(packed, values):
+        found = jnp.full_like(packed, 0) + values[0]
+        for r in range(1, rolls):
+            found = jnp.where(packed >= starts[r], values[r], found)
+        return found
+
+    row_code = packed_of(lax.broadcasted_iota(jnp.int32, (8, rows), 1))
+    codes[seq] = row_code
     pl.semaphore_wait(barrier, n_seq - 1 + n_voc - 1)
 
     def prompt_copy(j):
         peer = (seq + j) % n_seq
-        return remote(prompt_ref, pbuf.at[seq], p_s.at[j], p_r.at[seq], peer, voc)
+        return remote(pbuf.at[seq], pbuf.at[seq], p_s.at[j], p_r.at[seq], peer, voc)
 
     def code_copy(j):
         peer = (seq + j) % n_seq
-        return remote(row_ref, codes.at[seq], c_s.at[j], c_r.at[seq], peer, voc)
+        return remote(codes.at[seq], codes.at[seq], c_s.at[j], c_r.at[seq], peer, voc)
 
     def send_small(j, carry):
         prompt_copy(j).start()
@@ -168,6 +199,22 @@
 
     lax.fori_loop(1, n_seq, send_small, 0)
 
+    packed_col = packed_of(lax.broadcasted_iota(jnp.int32, (rows, 128), 0))
+    first_col = lookup(packed_col, starts)
+    prompt_col = lookup(packed_col, [prompt_of[r] for r in range(rolls)])
+    target_col = jnp.transpose(
+        jnp.broadcast_to(tgt_ref[...].reshape(1, rows).astype(F32), (128, rows))
+    ).astype(jnp.int32)
+    lane_col = lax.broadcasted_iota(jnp.int32, (rows, 128), 1)
+    col = jnp.where(lane_col == 0, first_col, packed_col)
+    col = jnp.where(lane_col == 2, prompt_col, col)
+    col_ref[...] = jnp.where(lane_col == 3, target_col, col)
+    place = packed_col - first_col + per_prompt * n_seq
+    angles = place.astype(F32) * freq_ref[...]
+    cos_ref[...] = jnp.cos(angles)
+    sine = jnp.sin(angles)
+    sin_ref[...] = jnp.where(lane_col < HD // 2, -sine, sine)
+
     def kv_copy(m, src, dst_seq, slot):
         return remote(kv.at[m, src], kv.at[m, src], kv_s.at[m, slot], kv_r.at[m, src], dst_seq, voc)
 
@@ -176,22 +223,22 @@
         return (values * cos_ref[...] + pltpu.roll(values, HD // 2, axis=1) * sin_ref[...]).astype(BF16)
 
     for m in range(2):
-        ing, qg, kg = ((ing_p, qg_p, kg_p), (ing_r, qg_r, kg_r))[m]
+        qg, kg = ((qg_p, kg_p), (qg_r, kg_r))[m]
         loads[4 * m].wait()
 
-        def norm_rows(i, carry, m=m, ing=ing):
+        def norm_rows(i, carry, m=m):
             here = pl.ds(pl.multiple_of(i * 32, 32), 32)
             values = hid[m, here, :].astype(F32)
             inv = lax.rsqrt(jnp.mean(values * values, axis=-1, keepdims=True) + EPSILON)
-            normed[here, :] = (values * inv * ing[...]).astype(BF16)
+            fin[0, here, :] = (values * inv * igain[m]).astype(BF16)
             return carry
 
         lax.fori_loop(0, rows // 32, norm_rows, 0)
         loads[4 * m + 1].wait()
         loads[4 * m + 2].wait()
-        key_rows = turn(dot(normed[...], wk[m]), kg[...])
+        key_rows = turn(dot(fin[0], wk[m]), kg[...])
         kv[m, seq, :, 0:HD] = key_rows
-        kv[m, seq, :, HD : 2 * HD] = dot(normed[...], wv[m]).astype(BF16)
+        kv[m, seq, :, HD : 2 * HD] = dot(fin[0], wv[m]).astype(BF16)
         kv_copy(m, seq, sibling, 0).start()
 
         def send_kv(j, carry, m=m):
@@ -201,14 +248,14 @@
         lax.fori_loop(1, n_chips, send_kv, 0)
         loads[4 * m + 3].wait()
         for h in range(0, heads, 2):
-            both = dot(normed[...], wq[m, :, h * HD : (h + 2) * HD])
+            both = dot(fin[0], wq[m, :, h * HD : (h + 2) * HD])
             query[m, h] = turn(both[:, :HD], qg[...])
             query[m, h + 1] = turn(both[:, HD:], qg[...])
 
     def wait_small(j, carry):
         src = (seq + n_seq - j) % n_seq
-        remote(prompt_ref, pbuf.at[src], p_s.at[j], p_r.at[src], src, voc).wait_recv()
-        remote(row_ref, codes.at[src], c_s.at[j], c_r.at[src], src, voc).wait_recv()
+        remote(pbuf.at[src], pbuf.at[src], p_s.at[j], p_r.at[src], src, voc).wait_recv()
+        remote(codes.at[src], codes.at[src], c_s.at[j], c_r.at[src], src, voc).wait_recv()
         prompt_copy(j).wait_send()
         code_copy(j).wait_send()
         return carry
@@ -220,25 +267,34 @@
     first = col_ref[:, 0:1]
     index = col_ref[:, 1:2]
     prompt = col_ref[:, 2:3]
-    prompt_rows = pbuf.shape[2]
-    per_prompt = prompt_rows // 4
-
-    def tile(m, src):
-        code = codes[src][0:1, :]
-        bias[...] = jnp.where((code >= first) & (code <= index), 0.0, NEGATIVE_FILL)
-
-        def head_step(h, carry):
-            scores = dot_t(query[m, h], kv[m, src, :, 0:HD]) * scale + bias[...]
-            old = mx_s[h]
-            new = jnp.maximum(old, jnp.max(scores, axis=-1, keepdims=True))
-            weights = jnp.exp(scores - new[:, 0:1])
-            factor = jnp.exp(old - new)
-            mx_s[h] = new
-            sum_s[h] = sum_s[h] * factor + jnp.sum(weights, axis=-1, keepdims=True)
-            acc[h] = acc[h] * factor + dot(weights.astype(BF16), kv[m, src, :, HD : 2 * HD])
-            return carry
-
-        lax.fori_loop(0, heads, head_step, 0, unroll=True)
+    prompt_all = n_seq * prompt_rows
+    tiles = prompt_all // rows
+    per_tile = rows // prompt_rows
+
+    def see(t, carry):
+        code = codes[t][0:1, :]
+        bias[t] = jnp.where((code >= first) & (code <= index), 0.0, NEGATIVE_FILL)
+        return carry
+
+    lax.fori_loop(0, n_seq, see, 0)
+    owner = (lax.broadcasted_iota(jnp.int32, (1, rows), 1) % prompt_rows) // per_prompt
+    bias[n_seq] = jnp.where(owner == prompt, 0.0, NEGATIVE_FILL)
+
+    def forward_kv(m):
+        def chip_step(j, inner):
+            src = ((chip + n_chips - j) % n_chips) * 2 + core
+            kv_copy(m, src, sibling, 0).wait_recv()
+            kv_copy(m, src, sibling, n_chips + j).start()
+            return inner
+
+        lax.fori_loop(1, n_chips, chip_step, 0)
+
+    def gathered_kv(m):
+        def chip_step(j, inner):
+            kv_copy(m, ((chip + n_chips - j) % n_chips) * 2 + (1 - core), sibling, 0).wait_recv()
+            return inner
+
+        lax.fori_loop(0, n_chips, chip_step, 0)
 
     is_end = (voc == 0) | (voc == n_voc - 1)
     middle = 1 + voc // 2
@@ -256,46 +312,63 @@
 
     def in_copy(k):
         m, here = k // chunks, rows_of(k, 0, CHUNK)
-        return remote(part.at[m, here, :], inbuf.at[m, here, :], in_s.at[k], in_r.at[k], seq, middle)
-
-    def attend(m, carry):
-        prompts = pbuf[:, m].reshape(n_seq * prompt_rows, 2 * HD)
-        owner = (lax.broadcasted_iota(jnp.int32, (1, n_seq * prompt_rows), 1) % prompt_rows) // per_prompt
-        cover = owner == prompt
+        return remote(inbuf.at[m, here, :], inbuf.at[m, here, :], in_s.at[k], in_r.at[k], seq, middle)
+
+    def prompt_tile(m, t):
+        here = pl.ds(t * per_tile, per_tile)
+        return pbuf[here, m].reshape(rows, 2 * HD)
+
+    def head_step(m, h):
+        rate = HD ** (-0.5)
+        q = query[m, h]
+
+        def seen(t, high):
+            scores = dot_t(q, kv[m, t, :, 0:HD]) + bias[t]
+            kept[t] = scores
+            return jnp.maximum(high, jnp.maximum(scores[:, :HD], scores[:, HD:]))
+
+        def seen_prompt(t, high):
+            scores = dot_t(q, prompt_tile(m, t)[:, 0:HD]) + bias[n_seq]
+            kept[n_seq + t] = scores
+            return jnp.maximum(high, jnp.maximum(scores[:, :HD], scores[:, HD:]))
+
+        high = jnp.full((rows, HD), NEGATIVE_FILL, F32)
+        high = lax.fori_loop(0, tiles, seen_prompt, high)
+        high = lax.fori_loop(0, n_seq, seen, high, unroll=2)
+        top = jnp.max(high, axis=-1, keepdims=True)
+
+        def weigh(t, values, state):
+            mass, total_value = state
+            weights = jnp.exp((kept[t] - top) * rate)
+            mass = mass + (weights[:, :HD] + weights[:, HD:])
+            return (mass, total_value + dot(weights.astype(BF16), values))
+
+        state = (jnp.zeros((rows, HD), F32), jnp.zeros((rows, HD), F32))
+        state = lax.fori_loop(
+            0, tiles, lambda t, c: weigh(n_seq + t, prompt_tile(m, t)[:, HD:], c), state
+        )
+        mass, value = lax.fori_loop(
+            0, n_seq, lambda t, c: weigh(t, kv[m, t, :, HD : 2 * HD], c), state, unroll=2
+        )
+        attended[m, :, h * HD : (h + 1) * HD] = (value / jnp.sum(mass, axis=-1, keepdims=True)).astype(BF16)
+
+    forward_kv(0)
+    gathered_kv(0)
+    for m in range(2):
+        if m == 1:
+            gathered_kv(1)
         for h in range(heads):
-            scores = jnp.where(cover, dot_t(query[m, h], prompts[:, :HD]) * scale, NEGATIVE_FILL)
-            top = jnp.max(scores, axis=-1, keepdims=True)
-            weights = jnp.exp(scores - top)
-            mx_s[h] = jnp.broadcast_to(top, (rows, HD))
-            sum_s[h] = jnp.broadcast_to(jnp.sum(weights, axis=-1, keepdims=True), (rows, HD))
-            acc[h] = dot(weights.astype(BF16), prompts[:, HD:])
-
-        tile(m, seq)
-        kv_copy(m, sibling, sibling, 0).wait_recv()
-        tile(m, sibling)
-
-        def chip_step(j, inner):
-            src_chip = (chip + n_chips - j) % n_chips
-            src = src_chip * 2 + core
-            kv_copy(m, src, sibling, 0).wait_recv()
-            kv_copy(m, src, sibling, n_chips + j).start()
-            tile(m, src)
-            src_sib = src_chip * 2 + (1 - core)
-            kv_copy(m, src_sib, sibling, 0).wait_recv()
-            tile(m, src_sib)
-            return inner
-
-        lax.fori_loop(1, n_chips, chip_step, 0)
-        for h in range(heads):
-            attended[m, :, h * HD : (h + 1) * HD] = (acc[h] / sum_s[h]).astype(BF16)
+            head_step(m, h)
+            if m == 0 and h == heads // 2:
+                forward_kv(1)
 
         @pl.when(is_end)
         def _():
-            def send_chunk(i, inner):
+            def send_chunk(i, inner, m=m):
                 k = m * chunks + i
 
                 def store(c, value):
-                    part[m, rows_of(k, 0, CHUNK), c : c + 512] = value.astype(BF16)
+                    inbuf[m, rows_of(k, 0, CHUNK), c : c + 512] = value.astype(BF16)
 
                 partial_chunk(k, store)
                 in_copy(k).start()
@@ -303,9 +376,6 @@
 
             lax.fori_loop(0, chunks, send_chunk, 0)
 
-        return carry
-
-    lax.fori_loop(0, 2, attend, 0)
     loads[10].wait()
     loads[11].wait()
 
@@ -366,7 +436,7 @@
 
             partial_chunk(k, store)
             pltpu.make_async_remote_copy(
-                src_ref=part.at[m, rows_of(k, 0, CHUNK), :],
+                src_ref=inbuf.at[m, rows_of(k, 0, CHUNK), :],
                 dst_ref=inbuf.at[m, rows_of(k, 0, CHUNK), :],
                 send_sem=in_s.at[k],
                 recv_sem=in_r.at[k],
@@ -377,22 +447,31 @@
             xs[k] = (own[away, :] + inbuf[m, rows_of(k, theirs, half), :].astype(F32)).astype(BF16)
             x_copy(k).start()
 
+            home = pl.ds(pl.multiple_of(mine, half), half)
+            keep[k % 2] = own[home, :] + inbuf[m, rows_of(k, mine, half), :].astype(F32)
+
             @pl.when(k > 0)
             def _():
-                pass_on(k - 1)
-
-            home = pl.ds(pl.multiple_of(mine, half), half)
-            here = rows_of(k, mine, half)
-            mixed = own[home, :] + inbuf[m, here, :].astype(F32)
+                complete(k - 1)
+
+            @pl.when(k > 1)
+            def _():
+                pass_on(k - 2)
+
+            return carry
+
+        def complete(k):
+            m, here = k // chunks, rows_of(k, mine, half)
             x_copy(k).wait_recv()
-            values = hid[m, here, :].astype(F32) + (mixed + xr[k].astype(F32))
+            values = hid[m, here, :].astype(F32) + (keep[k % 2] + xr[k].astype(F32))
             inv = lax.rsqrt(jnp.mean(values * values, axis=-1, keepdims=True) + EPSILON)
             fin[m, here, :] = (values * inv * fgain[m]).astype(BF16)
             f_copy(k, mine).start()
             e_copy(k, mine, 0).start()
-            return carry
 
         lax.fori_loop(0, total, step, 0)
+        complete(total - 1)
+        pass_on(total - 2)
         pass_on(total - 1)
 
         def drain(k, carry):
@@ -431,13 +510,14 @@
 
     diff = score(0) - score(1)
     diff_ref[...] = diff
-    per_token = diff / row_ref[2:3, :].astype(F32)
-    slot = row_ref[1:2, :]
+    packed_row = packed_of(lax.broadcasted_iota(jnp.int32, (1, rows), 1))
+    per_token = diff / lookup(packed_row, [lens[r] for r in range(rolls)]).astype(F32)
+    slot = lookup(packed_row, [jnp.int32(r) for r in range(rolls)])
     lane = lax.broadcasted_iota(jnp.int32, (8, 128), 1)
     block = jnp.zeros((8, 128), F32)
     for r in range(rolls):
         piece = jnp.sum(jnp.where(slot == r, per_token, 0.0), axis=1, keepdims=True)
-        block = jnp.where(lane == r, piece, block)
+        block = jnp.where(lane == slot_of[r], piece, block)
     rbuf[seq] = block
 
     def roll_copy(j):
@@ -505,33 +585,9 @@
     prompt_count, prefix_local = policy_prompt_keys.shape[:2]
     prompt_rows = prompt_count * prefix_local
 
-    slot_ids = jnp.arange(rows, dtype=jnp.int32)
-    packed = jnp.repeat(block_source, BLOCK) * BLOCK + slot_ids % BLOCK
-    ends = jnp.cumsum(lengths)
-    rollout = jnp.sum((packed[:, None] >= ends[None, :]).astype(jnp.int32), axis=1)
-    member = rollout[:, None] == jnp.arange(rolls, dtype=jnp.int32)[None, :]
-
-    def lookup(table):
-        return jnp.sum(jnp.where(member, table[None, :], 0), axis=1)
-
-    first = lookup(ends - lengths)
-    zero = jnp.zeros_like(packed)
-    col = jnp.stack([first, packed, lookup(rollout_prompt), targets], axis=1)
-    col = jnp.pad(col, ((0, 0), (0, 124)))
-    row = jnp.stack([packed, lookup(rollout_slot), lookup(lengths), zero, zero, zero, zero, zero], axis=0)
-    frequency = ROPE_BASE ** (-2.0 * jnp.arange(HD // 2, dtype=F32) / HD)
-    place = packed - first + prefix_local * n_seq
-    angles = place.astype(F32)[:, None] * frequency[None, :]
-    cosine, sine = jnp.cos(angles), jnp.sin(angles)
-    cosine = jnp.concatenate([cosine, cosine], axis=1)
-    sine = jnp.concatenate([-sine, sine], axis=1)
-
-    def both(keys, values):
-        return jnp.concatenate([keys.reshape(prompt_rows, HD), values.reshape(prompt_rows, HD)], axis=1)
-
-    prompts = jnp.stack(
-        [both(policy_prompt_keys, policy_prompt_values), both(reference_prompt_keys, reference_prompt_values)]
-    )
+    frequency = ROPE_BASE ** (-2.0 * np.arange(HD // 2, dtype=np.float32) / HD)
+    frequency = np.concatenate([frequency, frequency]).astype(np.float32)[None]
+    smem = pl.BlockSpec(memory_space=pltpu.SMEM)
     vmem = pl.BlockSpec(memory_space=pltpu.VMEM)
     hbm = pl.BlockSpec(memory_space=pl.ANY)
     dma = pltpu.SemaphoreType.DMA
@@ -542,7 +598,7 @@
             jax.ShapeDtypeStruct((1, rows), F32),
             jax.ShapeDtypeStruct((8, 128), F32),
         ),
-        in_specs=[vmem] * 5 + [hbm] * 2 + [vmem] * 8 + [hbm] * 10,
+        in_specs=[smem] * 4 + [vmem] * 6 + [hbm] * 2 + [vmem] * 8 + [hbm] * 10,
         out_specs=(vmem, vmem),
         scratch_shapes=[
             pltpu.VMEM((2, width, heads * HD), BF16),
@@ -552,21 +608,22 @@
             pltpu.VMEM((2, width, words), BF16),
             pltpu.VMEM((2, rows, width), BF16),
             pltpu.VMEM((2, 1, width), F32),
-            pltpu.VMEM((rows, width), BF16),
             pltpu.VMEM((2, heads, rows, HD), BF16),
             pltpu.VMEM((2, n_seq, rows, 2 * HD), BF16),
             pltpu.VMEM((n_seq, 2, prompt_rows, 2 * HD), BF16),
             pltpu.VMEM((n_seq, 8, rows), jnp.int32),
-            pltpu.VMEM((rows, rows), F32),
-            pltpu.VMEM((heads, rows, HD), F32),
-            pltpu.VMEM((heads, rows, HD), F32),
-            pltpu.VMEM((heads, rows, HD), F32),
+            pltpu.VMEM((n_seq + 1, rows, rows), F32),
+            pltpu.VMEM((n_seq + n_seq * prompt_rows // rows, rows, rows), F32),
+            pltpu.VMEM((rows, 128), jnp.int32),
+            pltpu.VMEM((rows, 128), F32),
+            pltpu.VMEM((rows, 128), F32),
+            pltpu.VMEM((2, 1, width), F32),
             pltpu.VMEM((2, rows, heads * HD), BF16),
-            pltpu.VMEM((2, rows, width), BF16),
             pltpu.VMEM((2, rows, width), BF16),
             pltpu.VMEM((total, CHUNK // 2, width), BF16),
             pltpu.VMEM((total, CHUNK // 2, width), BF16),
             pltpu.VMEM((CHUNK, width), F32),
+            pltpu.VMEM((2, CHUNK // 2, width), F32),
             pltpu.VMEM((2, rows, width), BF16),
             pltpu.VMEM((rows, 128), F32),
             pltpu.VMEM((4, 8, rows), F32),
@@ -595,21 +652,26 @@
             collective_id=0, has_side_effects=True, vmem_limit_bytes=60 * 1024 * 1024
         ),
     )(
-        col,
-        row,
-        cosine,
-        sine,
-        prompts,
+        lengths,
+        block_source,
+        rollout_prompt,
+        rollout_slot,
+        targets,
+        frequency,
+        policy_prompt_keys,
+        policy_prompt_values,
+        reference_prompt_keys,
+        reference_prompt_values,
         policy_hidden,
         reference_hidden,
-        policy_input_gain[None],
-        reference_input_gain[None],
+        policy_input_gain,
+        reference_input_gain,
         policy_query_gain[None],
         reference_query_gain[None],
         policy_key_gain[None],
         reference_key_gain[None],
-        policy_final_gain[None],
-        reference_final_gain[None],
+        policy_final_gain,
+        reference_final_gain,
         policy_query_weight,
         reference_query_weight,
         policy_key_weight,

time: 139 us -> 121 us (0.87)
  local copies, waits for them, and re-layouts: 9.13 us -> 2.4 us
  other arithmetic: 6.6 us -> 0 us
  Pallas kernels: 122 us -> 118 us
    broadcast_in_dim x5 -> x0, local copies, waits for them, and re-layouts: 5.3 us -> none  [the longest x1 1.31 us: local(): policy_input_gain[None]]
    pallas_call x1, Pallas kernels: 122 us -> 118 us  [local(): pl.pallas_call(functools.partial(kernel, n_seq, rolls), out_shape=(jax.Sh...]
    another operation x4 -> x0, other arithmetic: 2.87 us -> none  [the longest x2 1.36 us: local(): jnp.stack([both(policy_prompt_keys, policy_prompt_values), both(reference...]
where the time goes in v2:
time: 121 us
  Pallas kernels  118 us (98%)
  local copies, waits for them, and re-layouts  2.4 us (2%)
    pallas_call x1, Pallas kernels, local(): pl.pallas_call(functools.partial(kernel, n_seq, rolls), out_shape=(jax.Sh...  118 us

profile of v2, /device:TPU:0, one launch (start us, length us, event | category | flops | bytes accessed | tf_op | source)
XLA Modules:
  0.0 120.7 jit_solution(2130445647933640331)
XLA Ops:
  0.6 117.7 %shard_map.293 = (f32[1,256]{1,0:T(1,128)}, f32[8,128]{1,0:T(8,128)}) custom-call(s32[4]{0:T(128)} %lens.1, s32[2]{0:T(128)} %source.1, s32[4]{0:T(128)} %prompt_of.1, s32[4]{0:T(128)} %slot_of.1, s32[256]{0:T(256)} %tgt_ref.1, f32[1,128]{1,0:T(1,128)} %constant.2.clone.freq_ref, bf16[4,8,128]{2,1,0:T(8,128)(2,1)} %pk_p.1, bf16[4,8,128]{2,1,0:T(8,128)(2,1)} %pv_p.1, ...), custom_call_target="tpu_custom_call" | custom-call | tf_op jit(solution)/shard_map/pallas_call | solution.py:595
  118.3 1.2 slice_bitcast_fusion
  119.5 1.2 %copy.33 = f32[256]{0:T(256)} copy(f32[256]{0:T(256)} %bitcast.7) | data formatting | bytes 2048

commit v3 on v2

--- a/solution.py
+++ b/solution.py
@@ -81,10 +81,8 @@
     igain,
     attended,
     inbuf,
-    xs,
     xr,
     own,
-    keep,
     fin,
     stat,
     sbuf,
@@ -138,8 +136,9 @@
     )
     for i, (src, dst, m) in enumerate(order):
         copy = pltpu.make_async_copy(src, dst.at[m], w_sem.at[i])
+        loads.append(copy)
+    for copy in loads[:4]:
         copy.start()
-        loads.append(copy)
 
     barrier = pltpu.get_barrier_semaphore()
 
@@ -234,6 +233,8 @@
             return carry
 
         lax.fori_loop(0, rows // 32, norm_rows, 0)
+        for copy in loads[4 * (m + 1) : 4 * (m + 2)]:
+            copy.start()
         loads[4 * m + 1].wait()
         loads[4 * m + 2].wait()
         key_rows = turn(dot(fin[0], wk[m]), kg[...])
@@ -304,11 +305,10 @@
     def rows_of(k, off, count):
         return pl.ds(pl.multiple_of((k % chunks) * CHUNK + off, half), count)
 
-    def partial_chunk(k, store):
-        m = k // chunks
-        values = attended[m, rows_of(k, 0, CHUNK), :]
+    def partial_sums(m, out):
+        values = attended[m]
         for c in range(0, width, 512):
-            store(c, dot(values, wo[m, :, c : c + 512]))
+            out[m, :, c : c + 512] = dot(values, wo[m, :, c : c + 512]).astype(BF16)
 
     def in_copy(k):
         m, here = k // chunks, rows_of(k, 0, CHUNK)
@@ -363,30 +363,27 @@
                 forward_kv(1)
 
         @pl.when(is_end)
-        def _():
-            def send_chunk(i, inner, m=m):
-                k = m * chunks + i
-
-                def store(c, value):
-                    inbuf[m, rows_of(k, 0, CHUNK), c : c + 512] = value.astype(BF16)
-
-                partial_chunk(k, store)
-                in_copy(k).start()
-                return inner
-
-            lax.fori_loop(0, chunks, send_chunk, 0)
+        def _(m=m):
+            partial_sums(m, inbuf)
+            if m == 0:
+                in_copy(0).start()
+                in_copy(1).start()
+
+        @pl.when(jnp.logical_not(is_end))
+        def _(m=m):
+            partial_sums(m, own)
 
     loads[10].wait()
     loads[11].wait()
 
-    lanes = lax.broadcasted_iota(jnp.int32, (CHUNK, 128), 1)
-
-    def head_chunk(k):
-        m, here = k // chunks, rows_of(k, 0, CHUNK)
+    lanes = lax.broadcasted_iota(jnp.int32, (2 * CHUNK, 128), 1)
+
+    def head_pair(k):
+        m, here = k // chunks, rows_of(k, 0, 2 * CHUNK)
         logits = dot(fin[m, here, :], hd[m])
         top = jnp.max(logits, axis=-1, keepdims=True)
         mass = jnp.sum(jnp.exp(logits - top), axis=-1, keepdims=True)
-        word = voc * words + lax.broadcasted_iota(jnp.int32, (CHUNK, words), 1)
+        word = voc * words + lax.broadcasted_iota(jnp.int32, (2 * CHUNK, words), 1)
         target = col_ref[here, 3:4]
         hit = jnp.sum(jnp.where(word == target, logits, 0.0), axis=-1, keepdims=True)
         old = stat[here, :]
@@ -398,7 +395,7 @@
     theirs = half - mine
 
     def x_copy(k):
-        return remote(xs.at[k], xr.at[k], x_s.at[k], x_r.at[k], seq, other)
+        return remote(inbuf.at[k // chunks, rows_of(k, theirs, half), :], xr.at[k], x_s.at[k], x_r.at[k], seq, other)
 
     def f_copy(k, off):
         ref = fin.at[k // chunks, rows_of(k, off, half), :]
@@ -410,31 +407,41 @@
 
     @pl.when(is_end)
     def _():
-        def step(k, carry):
-            first_off = (middle - 1) * half
+        def issue(k, carry):
+            in_copy(k - 2).wait_send()
+            in_copy(k).start()
+            return carry
+
+        lax.fori_loop(2, total, issue, 0)
+        first_off = (middle - 1) * half
+
+        def landed(k):
             for which, off in ((0, first_off), (1, half - first_off)):
                 ref = fin.at[k // chunks, rows_of(k, off, half), :]
                 remote(ref, ref, e_s.at[2 * k + which], e_r.at[2 * k + which], seq, middle).wait_recv()
-            head_chunk(k)
-            in_copy(k).wait_send()
+
+        def step(i, carry):
+            landed(2 * i)
+            landed(2 * i + 1)
+            head_pair(2 * i)
             return carry
 
-        lax.fori_loop(0, total, step, 0)
+        lax.fori_loop(0, total // 2, step, 0)
+        in_copy(total - 2).wait_send()
+        in_copy(total - 1).wait_send()
 
     @pl.when(jnp.logical_not(is_end))
     def _():
         def pass_on(k):
             f_copy(k, theirs).wait_recv()
             e_copy(k, theirs, 1).start()
-            head_chunk(k)
+
+            @pl.when(k % 2 == 1)
+            def _():
+                head_pair(k - 1)
 
         def step(k, carry):
             m = k // chunks
-
-            def store(c, value):
-                own[:, c : c + 512] = value
-
-            partial_chunk(k, store)
             pltpu.make_async_remote_copy(
                 src_ref=inbuf.at[m, rows_of(k, 0, CHUNK), :],
                 dst_ref=inbuf.at[m, rows_of(k, 0, CHUNK), :],
@@ -443,12 +450,9 @@
                 device_id=(seq, end),
                 device_id_type=MESH,
             ).wait_recv()
-            away = pl.ds(pl.multiple_of(theirs, half), half)
-            xs[k] = (own[away, :] + inbuf[m, rows_of(k, theirs, half), :].astype(F32)).astype(BF16)
+            away = rows_of(k, theirs, half)
+            inbuf[m, away, :] = (own[m, away, :].astype(F32) + inbuf[m, away, :].astype(F32)).astype(BF16)
             x_copy(k).start()
-
-            home = pl.ds(pl.multiple_of(mine, half), half)
-            keep[k % 2] = own[home, :] + inbuf[m, rows_of(k, mine, half), :].astype(F32)
 
             @pl.when(k > 0)
             def _():
@@ -463,7 +467,8 @@
         def complete(k):
             m, here = k // chunks, rows_of(k, mine, half)
             x_copy(k).wait_recv()
-            values = hid[m, here, :].astype(F32) + (keep[k % 2] + xr[k].astype(F32))
+            mixed = own[m, here, :].astype(F32) + inbuf[m, here, :].astype(F32)
+            values = hid[m, here, :].astype(F32) + (mixed + xr[k].astype(F32))
             inv = lax.rsqrt(jnp.mean(values * values, axis=-1, keepdims=True) + EPSILON)
             fin[m, here, :] = (values * inv * fgain[m]).astype(BF16)
             f_copy(k, mine).start()
@@ -471,8 +476,8 @@
 
         lax.fori_loop(0, total, step, 0)
         complete(total - 1)
-        pass_on(total - 2)
-        pass_on(total - 1)
+        pass_on(jnp.int32(total - 2))
+        pass_on(jnp.int32(total - 1))
 
         def drain(k, carry):
             x_copy(k).wait_send()
@@ -509,7 +514,7 @@
         return hit - (top + jnp.log(mass))
 
     diff = score(0) - score(1)
-    diff_ref[...] = diff
+    diff_ref[...] = diff.reshape(rows)
     packed_row = packed_of(lax.broadcasted_iota(jnp.int32, (1, rows), 1))
     per_token = diff / lookup(packed_row, [lens[r] for r in range(rolls)]).astype(F32)
     slot = lookup(packed_row, [jnp.int32(r) for r in range(rolls)])
@@ -538,7 +543,9 @@
 
     lax.fori_loop(1, n_seq, start_roll, 0)
     lax.fori_loop(1, n_seq, wait_roll, 0)
-    mean_ref[...] = jnp.sum(rbuf[...], axis=0)
+    means = jnp.sum(rbuf[...], axis=0)
+    for r in range(rolls):
+        mean_ref[r] = means[0, r]
     lax.fori_loop(1, n_seq, drain_roll, 0)
     for j in range(1, n_voc):
         stat_copy(j).wait_send()
@@ -592,14 +599,14 @@
     hbm = pl.BlockSpec(memory_space=pl.ANY)
     dma = pltpu.SemaphoreType.DMA
     n_chips = n_seq // 2
-    diff, mean = pl.pallas_call(
+    return pl.pallas_call(
         functools.partial(kernel, n_seq, rolls),
         out_shape=(
-            jax.ShapeDtypeStruct((1, rows), F32),
-            jax.ShapeDtypeStruct((8, 128), F32),
+            jax.ShapeDtypeStruct((rows,), F32),
+            jax.ShapeDtypeStruct((rolls,), F32),
         ),
         in_specs=[smem] * 4 + [vmem] * 6 + [hbm] * 2 + [vmem] * 8 + [hbm] * 10,
-        out_specs=(vmem, vmem),
+        out_specs=(vmem, smem),
         scratch_shapes=[
             pltpu.VMEM((2, width, heads * HD), BF16),
             pltpu.VMEM((2, width, HD), BF16),
@@ -621,9 +628,7 @@
             pltpu.VMEM((2, rows, heads * HD), BF16),
             pltpu.VMEM((2, rows, width), BF16),
             pltpu.VMEM((total, CHUNK // 2, width), BF16),
-            pltpu.VMEM((total, CHUNK // 2, width), BF16),
-            pltpu.VMEM((CHUNK, width), F32),
-            pltpu.VMEM((2, CHUNK // 2, width), F32),
+            pltpu.VMEM((2, rows, width), BF16),
             pltpu.VMEM((2, rows, width), BF16),
             pltpu.VMEM((rows, 128), F32),
             pltpu.VMEM((4, 8, rows), F32),
@@ -683,7 +688,6 @@
         policy_head,
         reference_head,
     )
-    return (diff.reshape(rows), mean[0, :rolls])
 
 
 def solution(mesh):

time: 121 us -> 121 us (level)
  no operation moved by 1% of the time
where the time goes in v3:
time: 121 us
  Pallas kernels  118 us (98%)
  local copies, waits for them, and re-layouts  2.36 us (2%)
    pallas_call x1, Pallas kernels, local(): pl.pallas_call(functools.partial(kernel, n_seq, rolls), out_shape=(jax.Sh...  118 us

profile of v3, /device:TPU:0, one launch (start us, length us, event | category | flops | bytes accessed | tf_op | source)
XLA Modules:
  0.0 121.1 jit_solution(1889021191937999646)
XLA Ops:
  0.6 118.1 %shard_map.293 = (f32[256]{0:T(256)}, f32[4]{0:T(128)}) custom-call(s32[4]{0:T(128)} %lens.1, s32[2]{0:T(128)} %source.1, s32[4]{0:T(128)} %prompt_of.1, s32[4]{0:T(128)} %slot_of.1, s32[256]{0:T(256)} %tgt_ref.1, f32[1,128]{1,0:T(1,128)} %constant.2.clone.freq_ref, bf16[4,8,128]{2,1,0:T(8,128)(2,1)} %pk_p.1, bf16[4,8,128]{2,1,0:T(8,128)(2,1)} %pv_p.1, ...), custom_call_target="tpu_custom_call" | custom-call | tf_op jit(solution)/shard_map/pallas_call | solution.py:602
  118.7 1.2 %copy.34 = f32[256]{0:T(256)} copy(f32[256]{0:T(256)} %get-tuple-element.4) | data formatting | bytes 2048
  119.9 1.1 copy.35

commit v4 on v3

--- a/solution.py
+++ b/solution.py
@@ -13,7 +13,7 @@
 EPSILON = 1e-06
 ROPE_BASE = 1000000.0
 NEGATIVE_FILL = -1e30
-CHUNK = 64
+CHUNK = 32
 MESH = pl.DeviceIdType.MESH
 F32 = jnp.float32
 BF16 = jnp.bfloat16

time: 121 us -> 117 us (0.967)
  Pallas kernels: 118 us -> 114 us
    pallas_call x1, Pallas kernels: 118 us -> 114 us  [local(): pl.pallas_call(functools.partial(kernel, n_seq, rolls), out_shape=(jax.Sh...]
where the time goes in v4:
time: 117 us
  Pallas kernels  114 us (97%)
  local copies, waits for them, and re-layouts  2.36 us (2%)
    pallas_call x1, Pallas kernels, local(): pl.pallas_call(functools.partial(kernel, n_seq, rolls), out_shape=(jax.Sh...  114 us
    unnamed x2, local copies, waits for them, and re-layouts  2.36 us

profile of v4, /device:TPU:0, one launch (start us, length us, event | category | flops | bytes accessed | tf_op | source)
XLA Modules:
  0.0 117.0 jit_solution(2099884236336048226)
XLA Ops:
  0.6 114.0 %shard_map.293 = (f32[256]{0:T(256)}, f32[4]{0:T(128)}) custom-call(s32[4]{0:T(128)} %lens.1, s32[2]{0:T(128)} %source.1, s32[4]{0:T(128)} %prompt_of.1, s32[4]{0:T(128)} %slot_of.1, s32[256]{0:T(256)} %tgt_ref.1, f32[1,128]{1,0:T(1,128)} %constant.2.clone.freq_ref, bf16[4,8,128]{2,1,0:T(8,128)(2,1)} %pk_p.1, bf16[4,8,128]{2,1,0:T(8,128)(2,1)} %pv_p.1, ...), custom_call_target="tpu_custom_call" | custom-call | tf_op jit(solution)/shard_map/pallas_call | solution.py:602
  114.6 1.2 %copy.34 = f32[256]{0:T(256)} copy(f32[256]{0:T(256)} %get-tuple-element.4) | data formatting | bytes 2048
  115.8 1.1 copy.35
